TPU v7x, 128 devices: a whole 4x4x4 slice. The times are simulated.
128 devices in a mesh: ctx: 16 (over x, y_lo, core), head: 8 (over y_hi, z).
Axes of the slice: x: 4, y: 4 (y_hi: 2, y_lo: 2; y = y_hi * 2 + y_lo), z: 4, core: 2. Of those that a mesh axis runs over, the one named last changes fastest.
Arguments:
- q_nope: bfloat16 [4096, 4096], P('ctx', 'head'), may hold values from -5 to 5
- q_rope: bfloat16 [4096, 2048], P('ctx', 'head'), may hold values from -320 to 320
- latent: bfloat16 [4096, 512], P('ctx'), may hold values from -5 to 5
- rope_keys: bfloat16 [4096, 64], P('ctx'), may hold values from -4.5 to 4.5
- out_grad: bfloat16 [4096, 4096], P('ctx', 'head'), may hold values from -96 to 96
- up_keys: bfloat16 [512, 4096], P(None, 'head'), may hold values from -0.25 to 0.25
- up_values: bfloat16 [512, 4096], P(None, 'head'), may hold values from -0.25 to 0.25
- group_order: int32 [32], replicated, may hold values from 0 to 31, each once
Outputs:
- grad_q_nope: bfloat16 [4096, 4096], P('ctx', 'head')
- grad_q_rope: bfloat16 [4096, 2048], P('ctx', 'head')
- grad_latent: float32 [4096, 512], P('ctx')
- grad_rope: float32 [4096, 64], P('ctx')
- grad_up_keys: float32 [512, 4096], P('ctx', 'head')
- grad_up_values: float32 [512, 4096], P('ctx', 'head')
Inputs may be any that keep to these rules, and one draw needn't show every extreme that they name: `group_order`: each group place appears once.
All inputs are finite; a program needn't handle non-finite values.
Results may differ from a plain program's by a relative error of at most 0.0087.
Values may be sent and summed in bfloat16 or wider, within the bound.
A program may use at most 128 MiB of HBM per device.

v0:
```python
import math

import jax
import jax.numpy as jnp
from jax import lax
from jax.sharding import PartitionSpec as P

ROPE = 64
HEAD_DIM = 128
H_DEV = 4
GROUP = 128


NEG_LARGE = -1e30


def positions(group_order, first_row, count):
    rows = first_row + jnp.arange(count, dtype=jnp.int32)
    group_ids = rows // GROUP
    table = jnp.arange(group_order.shape[0], dtype=jnp.int32)
    placed = jnp.sum(
        jnp.where(group_ids[:, None] == table[None, :], group_order[None, :], 0), axis=1
    )
    return placed * GROUP + rows % GROUP


def per_device(q_nope, q_rope, latent, rope_keys, out_grad, up_keys, up_values, group_order):
    width = q_nope.shape[0]
    scale = (HEAD_DIM + ROPE) ** (-0.5)
    seq_len = lax.axis_size("ctx") * width
    q_pos = positions(group_order, lax.axis_index("ctx") * width, width)
    query_nope = q_nope.reshape(width, H_DEV, HEAD_DIM)
    query_rope = q_rope.reshape(width, H_DEV, ROPE)
    grad_heads = out_grad.reshape(width, H_DEV, HEAD_DIM)
    pair_cols = 2 * H_DEV * HEAD_DIM
    latent_all, rope_all = (
        lax.all_gather(latent, "ctx", axis=0, tiled=True),
        lax.all_gather(rope_keys, "ctx", axis=0, tiled=True),
    )
    keys_all = jnp.dot(latent_all, up_keys, preferred_element_type=jnp.float32).astype(jnp.bfloat16)
    values_all = jnp.dot(latent_all, up_values, preferred_element_type=jnp.float32).astype(
        jnp.bfloat16
    )

    def fetch(start, count):
        key_rows = lax.dynamic_slice_in_dim(keys_all, start, count, 0).reshape(
            count, H_DEV, HEAD_DIM
        )
        value_rows = lax.dynamic_slice_in_dim(values_all, start, count, 0).reshape(
            count, H_DEV, HEAD_DIM
        )
        rope_rows = lax.dynamic_slice_in_dim(rope_all, start, count, 0)
        return (key_rows, value_rows, rope_rows)

    def block_scores(key_rows, rope_rows, k_pos):
        raw = jnp.einsum("thd,khd->htk", query_nope, key_rows, preferred_element_type=jnp.float32)
        raw = raw + jnp.einsum(
            "thr,kr->htk", query_rope, rope_rows, preferred_element_type=jnp.float32
        )
        visible = (k_pos[None, :] <= q_pos[:, None])[None]
        return (jnp.where(visible, raw * scale, NEG_LARGE), visible)

    block = math.gcd(seq_len, 512)
    block_count = seq_len // block

    def stats_visit(carry, index):
        start = index * block
        k_pos = positions(group_order, start, block)
        row_top, row_total, weighted = carry
        key_rows, value_rows, rope_rows = fetch(start, block)
        score, visible = block_scores(key_rows, rope_rows, k_pos)
        dattn = jnp.einsum(
            "thd,khd->htk", grad_heads, value_rows, preferred_element_type=jnp.float32
        )
        new_top = jnp.maximum(row_top, jnp.max(score, axis=2))
        factor = jnp.exp(row_top - new_top)
        expd = jnp.where(visible, jnp.exp(score - new_top[..., None]), 0.0)
        new_total = row_total * factor + jnp.sum(expd, axis=2)
        new_weighted = weighted * factor + jnp.sum(expd * dattn, axis=2)
        carry = (new_top, new_total, new_weighted)
        return (carry, None)

    start_top = jnp.full((H_DEV, width), NEG_LARGE, jnp.float32)
    zeros_rows = jnp.zeros((H_DEV, width), jnp.float32)
    row_top, row_total, weighted = lax.scan(
        stats_visit, (start_top, zeros_rows, zeros_rows), jnp.arange(block_count, dtype=jnp.int32)
    )[0]
    delta = weighted / row_total

    def grad_visit(carry, index):
        start = index * block
        k_pos = positions(group_order, start, block)
        acc_nope, acc_rope = carry
        key_rows, value_rows, rope_rows = fetch(start, block)
        score, visible = block_scores(key_rows, rope_rows, k_pos)
        attn = jnp.where(visible, jnp.exp(score - row_top[..., None]) / row_total[..., None], 0.0)
        dattn = jnp.einsum(
            "thd,khd->htk", grad_heads, value_rows, preferred_element_type=jnp.float32
        )
        dscore = (attn * (dattn - delta[..., None])).astype(jnp.bfloat16)
        acc_nope = acc_nope + jnp.einsum(
            "htk,khd->thd", dscore, key_rows, preferred_element_type=jnp.float32
        )
        acc_rope = acc_rope + jnp.einsum(
            "htk,kr->thr", dscore, rope_rows, preferred_element_type=jnp.float32
        )
        dkey = (
            jnp.einsum("htk,thd->khd", dscore, query_nope, preferred_element_type=jnp.float32)
            * scale
        )
        dvalue = jnp.einsum(
            "htk,thd->khd",
            attn.astype(jnp.bfloat16),
            grad_heads,
            preferred_element_type=jnp.float32,
        )
        drope = (
            jnp.einsum("htk,thr->kr", dscore, query_rope, preferred_element_type=jnp.float32)
            * scale
        )
        pair_terms = jnp.stack([dkey, dvalue], axis=1).reshape(block, pair_cols)
        return ((acc_nope, acc_rope), (pair_terms, drope))

    start_nope = jnp.zeros((width, H_DEV, HEAD_DIM), jnp.float32)
    start_rope = jnp.zeros((width, H_DEV, ROPE), jnp.float32)
    (acc_nope, acc_rope), (pair_stack, rope_stack) = lax.scan(
        grad_visit, (start_nope, start_rope), jnp.arange(block_count, dtype=jnp.int32)
    )
    grad_q_nope = (acc_nope * scale).astype(jnp.bfloat16).reshape(width, H_DEV * HEAD_DIM)
    grad_q_rope = (acc_rope * scale).astype(jnp.bfloat16).reshape(width, H_DEV * ROPE)
    pair_sum, rope_part = (
        lax.psum_scatter(
            pair_stack.reshape(seq_len, pair_cols), "ctx", scatter_dimension=0, tiled=True
        ),
        lax.psum_scatter(rope_stack.reshape(seq_len, ROPE), "ctx", scatter_dimension=0, tiled=True),
    )
    pair_sum = pair_sum.reshape(width, 2, H_DEV * HEAD_DIM)
    dkeys = pair_sum[:, 0].astype(jnp.bfloat16)
    dvalues = pair_sum[:, 1].astype(jnp.bfloat16)
    contract_cols = (((1,), (1,)), ((), ()))
    latent_part = lax.dot_general(dkeys, up_keys, contract_cols, preferred_element_type=jnp.float32)
    latent_part = latent_part + lax.dot_general(
        dvalues, up_values, contract_cols, preferred_element_type=jnp.float32
    )
    grad_latent, grad_rope = lax.psum((latent_part, rope_part), "head")
    contract_rows = (((0,), (0,)), ((), ()))
    weight_keys = lax.dot_general(latent, dkeys, contract_rows, preferred_element_type=jnp.float32)
    weight_values = lax.dot_general(
        latent, dvalues, contract_rows, preferred_element_type=jnp.float32
    )
    grad_up_keys, grad_up_values = (
        lax.psum_scatter(weight_keys, "ctx", scatter_dimension=0, tiled=True),
        lax.psum_scatter(weight_values, "ctx", scatter_dimension=0, tiled=True),
    )
    return (grad_q_nope, grad_q_rope, grad_latent, grad_rope, grad_up_keys, grad_up_values)


def solution(mesh):
    in_specs = (
        P("ctx", "head"),
        P("ctx", "head"),
        P("ctx", None),
        P("ctx", None),
        P("ctx", "head"),
        P(None, "head"),
        P(None, "head"),
        P(),
    )
    out_specs = (
        P("ctx", "head"),
        P("ctx", "head"),
        P("ctx", None),
        P("ctx", None),
        P("ctx", "head"),
        P("ctx", "head"),
    )
    return jax.shard_map(
        per_device, mesh=mesh, in_specs=in_specs, out_specs=out_specs, check_vma=False
    )
```

profile of v0, /device:TPU:0, one launch (start us, length us, event | category | flops | bytes accessed | tf_op | source)
XLA Modules:
  0.0 750.5 jit_solution(6171262483542442688)
XLA Ops:
  11.8 22.9 %all_gather.7 = bf16[4096,64]{0,1:T(8,128)(2,1)} all-gather(bf16[256,64]{0,1:T(8,128)(2,1)S(1)} %copy-done.6), channel_id=1, replica_groups=mesh['ctx'=16,'head'=8] {'ctx'}, dimensions={0}, use_global_device_ids=true | all-gather | bytes 557056 | tf_op jit(solution)/shard_map/all_gather | solution.py:38
  34.7 15.2 %all-gather.2.cloned.1.call-done = bf16[4096,512]{1,0:T(8,128)(2,1)} async-done(((bf16[256,512]{1,0:T(8,128)(2,1)}), bf16[4096,512]{1,0:T(8,128)(2,1)}) %all-gather.2.cloned.1.call-update) | async-done | bytes 4194320 | tf_op jit(solution)/shard_map/all_gather | solution.py:37
  49.9 6.5 convolution_convert_fusion
  56.4 6.4 copy.104
  62.7 6.5 convolution_convert_fusion.1
  69.2 6.4 copy.106
  75.6 47.8 %while.36 = (s32[]{:T(128)}, f32[4,256]{1,0:T(4,128)S(1)}, f32[4,256]{1,0:T(4,128)S(1)}, f32[4,256]{1,0:T(4,128)S(1)}, s32[8]{0:T(128)S(1)}, /*index=5*/s32[32]{...) while((s32[]{:T(128)}, f32[4,256]{1,0:T(4,128)S(1)}, ...), condition=%wide.region_6.7_spmd.clone, body=%wide.region_1.6_spmd.clone.sunk | while | flops 341513728 | bytes 14964090 | solution.py:85
  123.5 158.1 %while.37 = (s32[]{:T(128)}, f32[256,4,128]{0,2,1:T(8,128)}, f32[256,4,64]{0,2,1:T(8,128)}, f32[8,512,1024]{2,1,0:T(8,128)}, f32[8,512,64]{1,0,2:T(8,128)}, /*in...) while((s32[]{:T(128)}, f32[256,4,128]{0,2,1:T(8,128)}, ...), condition=%wide.region_9.10_spmd.clone, body=%wide.region_7.9_spmd.clone.sunk | while | flops 879065600 | bytes 38036900 | solution.py:126
  137.0 3.8 dynamic_update_slice.20
  148.2 2.2 fusion.135
  151.0 2.0 fusion.136
  156.9 3.8 dynamic_update_slice.20
  168.1 2.2 fusion.135
  176.8 3.8 dynamic_update_slice.20
  188.0 2.2 fusion.135
  196.7 3.8 dynamic_update_slice.20
  207.9 2.2 fusion.135
  210.7 2.0 fusion.136
  216.6 3.8 dynamic_update_slice.20
  227.9 2.2 fusion.135
  230.6 2.0 fusion.136
  236.6 3.8 dynamic_update_slice.20
  247.8 2.2 fusion.135
  250.5 2.0 fusion.136
  256.5 3.8 dynamic_update_slice.20
  267.7 2.2 fusion.135
  276.4 3.8 dynamic_update_slice.20
  284.5 174.1 %reduce-scatter.9.cloned.1.call-done = f32[256,1024]{1,0:T(8,128)} async-done(((f32[4096,1024]{1,0:T(8,128)}), f32[256,1024]{1,0:T(8,128)}) %reduce-scatter.9.cloned.1.call-update) | async-done | bytes 1048592 | tf_op jit(solution)/shard_map/reduce_scatter | solution.py:132
  462.5 65.2 %reduce-scatter.11.cloned.1.call-done = f32[256,64]{0,1:T(8,128)} async-done(((f32[4096,64]{0,1:T(8,128)}), f32[256,64]{0,1:T(8,128)}) %reduce-scatter.11.cloned.1.call-update) | async-done | bytes 65552 | tf_op jit(solution)/shard_map/reduce_scatter | solution.py:135
  535.0 80.0 %all-reduce.3.cloned.1.call-done = (f32[256,512]{1,0:T(8,128)}, f32[256,64]{0,1:T(8,128)}) async-done(((f32[256,512]{1,0:T(8,128)}, f32[256,64]{0,1:T(8,128)}), (f32[256,512]{1,0:T(8,128)}, f32[256,64]{0,1:T(8,128)})) %all-reduce.3.cloned.1.call-update) | async-done | bytes 589840 | tf_op jit(solution)/shard_map/psum | solution.py:145
  615.0 62.4 %reduce-scatter.15.cloned.1.call-done = f32[32,512]{1,0:T(8,128)} async-done(((f32[512,512]{1,0:T(8,128)}), f32[32,512]{1,0:T(8,128)}) %reduce-scatter.15.cloned.1.call-update) | async-done | bytes 65552
  677.4 62.9 %reduce-scatter.13.cloned.1.call-done = f32[32,512]{1,0:T(8,128)} async-done(((f32[512,512]{1,0:T(8,128)}), f32[32,512]{1,0:T(8,128)}) %reduce-scatter.13.cloned.1.call-update) | async-done | bytes 65552
  (297 shorter events, 162.8 us)
Async XLA Ops:
  7.2 55.6 %copy-start = (bf16[512,512]{1,0:T(8,128)(2,1)S(1)}, bf16[512,512]{1,0:T(8,128)(2,1)}, u32[]{:S(2)}) copy-start(bf16[512,512]{1,0:T(8,128)(2,1)} %param.17) | copy-start | bytes 1572868
  7.2 4.5 copy-start.5
  7.2 4.6 copy-start.6
  7.2 42.7 %copy-start.3 = (bf16[512,512]{1,0:T(8,128)(2,1)S(1)}, bf16[512,512]{1,0:T(8,128)(2,1)}, u32[]{:S(2)}) copy-start(bf16[512,512]{1,0:T(8,128)(2,1)} %param.18) | copy-start | bytes 1572868
  7.2 42.7 %all-gather.2.cloned.1.call-start = ((), (), s32[]{:S(2)}) async-start(), calls=%async_computation.4 | async-start | bytes 4456448 | tf_op jit(solution)/shard_map/all_gather | solution.py:37
  7.9 450.6 %reduce-scatter.9.cloned.1.call-start = ((), (), s32[]{:S(2)}) async-start(), calls=%async_computation.5 | async-start | bytes 17825792 | tf_op jit(solution)/shard_map/reduce_scatter | solution.py:132
  281.6 1.2 copy-start.2
  281.6 246.1 %reduce-scatter.11.cloned.1.call-start = ((), (), s32[]{:S(2)}) async-start(), calls=%async_computation.6 | async-start | bytes 1114112 | tf_op jit(solution)/shard_map/reduce_scatter | solution.py:135
  284.5 330.5 %all-reduce.3.cloned.1.call-start = ((), (), s32[]{:S(2)}) async-start(), calls=%async_computation.9 | async-start | bytes 1179648 | tf_op jit(solution)/shard_map/psum | solution.py:145
  459.9 1.5 copy-start.4
  461.0 66.8 %copy-start.1 = (bf16[256,512]{1,0:T(8,128)(2,1)S(1)}, bf16[256,512]{1,0:T(8,128)(2,1)}, u32[]{:S(2)}) copy-start(bf16[256,512]{1,0:T(8,128)(2,1)} %param.14) | copy-start | bytes 786436
  527.8 149.6 %reduce-scatter.15.cloned.1.call-start = ((), (), s32[]{:S(2)}) async-start(), calls=%async_computation.8 | async-start | bytes 1114112
  529.6 210.8 %reduce-scatter.13.cloned.1.call-start = ((), (), s32[]{:S(2)}) async-start(), calls=%async_computation.7 | async-start | bytes 1114112
Sparse Core Ops, SparseCore 0:
  9.8 40.0 all-gather.1
  281.8 176.7 reduce-scatter.8
  461.0 66.7 reduce-scatter.10
  530.3 84.6 all-reduce.2
  617.9 59.4 reduce-scatter.14
  680.2 60.1 reduce-scatter.12
where the time goes:
time: 754 us; the launch traced here: 751 us
  waiting for transfers between devices  461 us (61%)
  local copies, waits for them, and re-layouts  116 us (15%)
  matrix products  102 us (14%)
  other arithmetic  23.3 us (3%)
  blocking collectives  22.9 us (3%)
  between operations  14.4 us (2%)
  loops' own time  11.6 us (2%)
    reduce_scatter x1, waiting for transfers between devices, per_device(): lax.psum_scatter(pair_stack.reshape(seq_len, pair_cols), 'ctx', scatter_d...  174 us
    unnamed x8, waiting for transfers between devices  126 us
    psum x1, waiting for transfers between devices, per_device(): grad_latent, grad_rope = lax.psum((latent_part, rope_part), 'head')  80 us
    reduce_scatter x1, waiting for transfers between devices, per_device(): lax.psum_scatter(rope_stack.reshape(seq_len, ROPE), 'ctx', scatter_dimens...  65.2 us
    dynamic_update_slice x32, local copies, waits for them, and re-layouts, per_device(): lax.scan(grad_visit, (start_nope, start_rope), jnp.arange(block_count, dt...  58.2 us
    unnamed x27, local copies, waits for them, and re-layouts  25.7 us
    dot_general x16, matrix products, block_scores(): jnp.einsum('thr,kr->htk', query_rope, rope_rows, preferred_element_type=j...  25.4 us
    all_gather x1, blocking collectives, per_device(): lax.all_gather(rope_keys, 'ctx', axis=0, tiled=True)  22.9 us
  transfers between devices with their start and end apart: 6, of which 6 were waited for; matrix products, arithmetic and copies ran while one was open for 2% of the time, Pallas kernels for 0%

commit v1 on v0

v1 whole, which is shorter than its diff:
```python
import functools
import math

import jax
import jax.numpy as jnp
from jax import lax
from jax.experimental import pallas as pl
from jax.experimental.pallas import tpu as pltpu
from jax.sharding import PartitionSpec as P

MESH = pl.DeviceIdType.MESH
F32 = jnp.float32
BF16 = jnp.bfloat16

SCALE = (128 + 64) ** (-0.5)
EXP2_SCALE = SCALE * math.log2(math.e)
NEG_LARGE = -1e30

GROUP = 128
GROUPS = 32
BLOCKS = 16
TOKENS = 256
ROWS = 640
DQ_ROWS = 384
CHUNK = 512
PAIR = 256
MIB = 1024 * 1024

NT = (((1,), (1,)), ((), ()))
TN = (((0,), (0,)), ((), ()))


def low_lanes(rows):
    return lax.broadcasted_iota(jnp.int32, (rows, 128), 1) < 64


def swap_halves(tile):
    return pltpu.roll(tile, 64, 1)


def place_of(me):
    x = lax.div(me, 4)
    quarter = lax.rem(me, 4)
    core = lax.rem(quarter, 2)
    y = lax.div(quarter, 2)
    y_mate = 4 * x + 2 * (1 - y) + core
    core_mate = 4 * x + 2 * y + (1 - core)
    return x, quarter, y, core, y_mate, core_mate


def remote(src, dst, send_sem, recv_sem, ctx):
    return pltpu.make_async_remote_copy(
        src_ref=src,
        dst_ref=dst,
        send_sem=send_sem,
        recv_sem=recv_sem,
        device_id={"ctx": ctx},
        device_id_type=MESH,
    )


def exchange_kernel(
    qn, qr, og, lat, rope, uk, uv, kv, qd,
    skv, sq, send_x, send_y, send_c, recv_kv, send_q, recv_q, local_sem,
):
    me = lax.axis_index("ctx")
    x, quarter, y, core, y_mate, core_mate = place_of(me)
    barrier = pltpu.get_barrier_semaphore()
    for o in (1, 2, 3):
        pl.semaphore_signal(
            barrier, inc=1, device_id={"ctx": 4 * lax.rem(x + o, 4) + quarter}, device_id_type=MESH
        )
    for mate in (y_mate, core_mate):
        pl.semaphore_signal(barrier, inc=1, device_id={"ctx": mate}, device_id_type=MESH)

    keys = jnp.dot(lat[...], uk[...], preferred_element_type=F32).astype(BF16)
    values = jnp.dot(lat[...], uv[...], preferred_element_type=F32).astype(BF16)
    rope_packed = jnp.concatenate([rope[0:128, :], rope[128:256, :]], axis=1)
    for h in range(4):
        skv[h, 0:256, :] = keys[:, 128 * h : 128 * h + 128]
        skv[h, 256:512, :] = values[:, 128 * h : 128 * h + 128]
        skv[h, 512:640, :] = rope_packed
    pl.semaphore_wait(barrier, 5)

    started = []
    for o in (1, 3, 2):
        other = lax.rem(x + o, 4)
        started.append(
            remote(skv.at[other], kv.at[me], send_x.at[o - 1], recv_kv.at[me], 4 * other + quarter)
        )
        started[-1].start()
    own = pltpu.make_async_copy(skv.at[x], kv.at[me], local_sem.at[0])
    own.start()
    started.append(remote(skv.at[x], kv.at[me], send_y.at[0], recv_kv.at[me], y_mate))
    started[-1].start()
    started.append(remote(skv.at[x], kv.at[me], send_c.at[0], recv_kv.at[me], core_mate))
    started[-1].start()

    low = low_lanes(128)
    for h in range(4):
        sq[h, 0:256, :] = qn[:, 128 * h : 128 * h + 128]
        sq[h, 256:512, :] = og[:, 128 * h : 128 * h + 128]
        tile = qr[:, 128 * (h // 2) : 128 * (h // 2) + 128].astype(F32)
        top, bottom = tile[0:128], tile[128:256]
        if h % 2 == 0:
            packed = jnp.where(low, top, swap_halves(bottom))
        else:
            packed = jnp.where(low, swap_halves(top), bottom)
        sq[h, 512:640, :] = packed.astype(BF16)
    for o in (1, 3, 2):
        other = lax.rem(x + o, 4)
        started.append(
            remote(sq.at[other], qd.at[x], send_q.at[o - 1], recv_q.at[x], 4 * other + quarter)
        )
        started[-1].start()
    own_q = pltpu.make_async_copy(sq.at[x], qd.at[x], local_sem.at[1])
    own_q.start()

    def arrived(block):
        remote(kv.at[block], kv.at[block], send_c.at[0], recv_kv.at[block], core_mate).wait_recv()

    for n, o in enumerate((1, 3, 2)):
        block = 4 * lax.rem(x + o, 4) + quarter
        arrived(block)
        started.append(
            remote(kv.at[block], kv.at[block], send_y.at[n + 1], recv_kv.at[block], y_mate)
        )
        started[-1].start()
        started.append(
            remote(kv.at[block], kv.at[block], send_c.at[n + 1], recv_kv.at[block], core_mate)
        )
        started[-1].start()
    for n, o in enumerate((0, 1, 3, 2)):
        block = 4 * lax.rem(x + o, 4) + 2 * (1 - y) + core
        arrived(block)
        started.append(
            remote(kv.at[block], kv.at[block], send_c.at[n + 4], recv_kv.at[block], core_mate)
        )
        started[-1].start()
    for o in range(4):
        for side in range(2):
            arrived(4 * o + 2 * side + (1 - core))
    for o in (1, 3, 2):
        other = lax.rem(x + o, 4)
        remote(sq.at[other], qd.at[other], send_q.at[0], recv_q.at[other], core_mate).wait_recv()
    own.wait()
    own_q.wait()
    for copy in started:
        copy.wait_send()


def exchange(qn, qr, og, lat, rope, uk, uv):
    vmem = pl.BlockSpec(memory_space=pltpu.VMEM)
    anywhere = pl.BlockSpec(memory_space=pl.ANY)
    return pl.pallas_call(
        exchange_kernel,
        name="exchange",
        out_shape=(
            jax.ShapeDtypeStruct((BLOCKS, ROWS, 128), BF16),
            jax.ShapeDtypeStruct((4, ROWS, 128), BF16),
        ),
        in_specs=[vmem] * 7,
        out_specs=(anywhere, anywhere),
        scratch_shapes=[
            pltpu.VMEM((4, ROWS, 128), BF16),
            pltpu.VMEM((4, ROWS, 128), BF16),
            pltpu.SemaphoreType.DMA((3,)),
            pltpu.SemaphoreType.DMA((4,)),
            pltpu.SemaphoreType.DMA((8,)),
            pltpu.SemaphoreType.DMA((BLOCKS,)),
            pltpu.SemaphoreType.DMA((3,)),
            pltpu.SemaphoreType.DMA((4,)),
            pltpu.SemaphoreType.DMA((2,)),
        ],
        compiler_params=pltpu.CompilerParams(
            collective_id=0, has_side_effects=True, vmem_limit_bytes=32 * MIB
        ),
    )(qn, qr, og, lat, rope, uk, uv)


def attention_kernel(
    order, kv, qd, dkv, dq,
    held, q_place, q_group, kc, kt, vc, rp, qc, qct, doc, doct, s_all, dp_all, dkc, dvc, dqt,
    dq_rope, dk_rope, sems,
):
    quarter = lax.rem(lax.axis_index("ctx"), 4)

    @pl.loop(0, GROUPS)
    def _(g):
        held[order[g]] = g

    def load_copies(p):
        g = held[p]
        block, row = lax.div(g, 2), pl.multiple_of(lax.rem(g, 2) * GROUP, GROUP)
        to = pl.ds(pl.multiple_of(p * GROUP, GROUP), GROUP)
        return (
            pltpu.make_async_copy(
                kv.at[block, pl.ds(row, GROUP), :], kc.at[to, pl.ds(0, 128)], sems.at[0, p]
            ),
            pltpu.make_async_copy(kv.at[block, pl.ds(256 + row, GROUP), :], vc.at[to, :], sems.at[1, p]),
            pltpu.make_async_copy(kv.at[block, pl.ds(512, GROUP), :], rp.at[to, :], sems.at[2, p]),
        )

    @pl.loop(0, GROUPS)
    def _(p):
        for copy in load_copies(p):
            copy.start()

    q_place[8] = 0

    @pl.loop(0, GROUPS, init_carry=jnp.int32(0))
    def _(p, n):
        g = held[p]
        mine = lax.rem(lax.div(g, 2), 4) == quarter
        q_place[n] = p
        q_group[n] = g
        return n + jnp.where(mine, 1, 0)

    low = low_lanes(GROUP)
    low_int = low.astype(jnp.int32)

    @pl.loop(0, 8)
    def _(n):
        g = q_group[n]
        slot, half = lax.div(g, 8), lax.rem(g, 2)
        row = pl.multiple_of(half * GROUP, GROUP)
        to = pl.ds(pl.multiple_of(n * GROUP, GROUP), GROUP)
        qc[to, 0:128] = qd[slot, pl.ds(row, GROUP), :]
        doc[to, :] = qd[slot, pl.ds(256 + row, GROUP), :]
        packed = qd[slot, 512:640, :].astype(F32)
        keep = low_int == 1 - half
        qc[to, 128:256] = jnp.where(keep, packed, swap_halves(packed)).astype(BF16)

    @pl.loop(0, GROUPS * GROUP // CHUNK)
    def _(c):
        rows = pl.ds(pl.multiple_of(c * CHUNK, CHUNK), CHUNK)
        dkc[rows, :] = jnp.zeros((CHUNK, 256), F32)
        dvc[rows, :] = jnp.zeros((CHUNK, 128), F32)

    for i in range(4):
        qct[i] = qc[PAIR * i : PAIR * i + PAIR, :].T
        doct[i] = doc[PAIR * i : PAIR * i + PAIR, :].T

    @pl.loop(0, GROUPS)
    def _(p):
        for copy in load_copies(p):
            copy.wait()
        half = lax.rem(held[p], 2)
        to = pl.ds(pl.multiple_of(p * GROUP, GROUP), GROUP)
        keep = low_int == 1 - half
        rope = jnp.where(keep, rp[to, :].astype(F32), 0.0).astype(BF16)
        kc[to, 128:256] = rope
        kt[p, 0:128, :] = kc[to, 0:128].T
        kt[p, 128:256, :] = rope.T

    row_iota = lax.broadcasted_iota(jnp.int32, (CHUNK, PAIR), 0)
    lane_iota = lax.broadcasted_iota(jnp.int32, (1, PAIR), 1)

    def by_eights(block):
        return block.reshape(CHUNK // 8, 8, PAIR)

    @pl.loop(0, 4)
    def _(i):
        place_a, place_b = q_place[2 * i], q_place[2 * i + 1]
        whole = lax.div(place_a, CHUNK // GROUP)
        count = lax.div(place_b, CHUNK // GROUP) + 1
        q_pos = jnp.where(
            lane_iota < GROUP, place_a * GROUP + lane_iota, (place_b - 1) * GROUP + lane_iota
        )
        q_rows = pl.ds(pl.multiple_of(i * PAIR, PAIR), PAIR)

        def scores(c, top, masked):
            rows = pl.ds(pl.multiple_of(c * CHUNK, CHUNK), CHUNK)
            s = jnp.dot(kc[rows, :], qct[i], preferred_element_type=F32)
            if masked:
                s = jnp.where(row_iota + c * CHUNK <= q_pos, s, NEG_LARGE)
            s_all[rows, :] = s
            dp_all[rows, :] = jnp.dot(vc[rows, :], doct[i], preferred_element_type=F32)
            return jnp.maximum(top, jnp.max(by_eights(s), axis=0))

        top = jnp.full((8, PAIR), NEG_LARGE, F32)
        top = lax.fori_loop(0, whole, lambda c, t: scores(c, t, False), top)
        top = lax.fori_loop(whole, count, lambda c, t: scores(c, t, True), top)
        top = jnp.max(top, axis=0, keepdims=True)

        def exps(c, carry):
            total, weighted = carry
            rows = pl.ds(pl.multiple_of(c * CHUNK, CHUNK), CHUNK)
            p = jnp.exp2((s_all[rows, :] - top) * EXP2_SCALE)
            s_all[rows, :] = p
            total = total + jnp.sum(by_eights(p), axis=0)
            weighted = weighted + jnp.sum(by_eights(p * dp_all[rows, :]), axis=0)
            return total, weighted

        zeros = jnp.zeros((8, PAIR), F32)
        total, weighted = lax.fori_loop(0, count, exps, (zeros, zeros))
        inverse = 1.0 / jnp.sum(total, axis=0, keepdims=True)
        delta = jnp.sum(weighted, axis=0, keepdims=True) * inverse
        dqt[...] = jnp.zeros((256, PAIR), F32)

        def grads(c, carry):
            rows = pl.ds(pl.multiple_of(c * CHUNK, CHUNK), CHUNK)
            attn = s_all[rows, :] * inverse
            ds = (attn * (dp_all[rows, :] - delta)).astype(BF16)
            dvc[rows, :] += jnp.dot(attn.astype(BF16), doc[q_rows, :], preferred_element_type=F32)
            dkc[rows, :] += jnp.dot(ds, qc[q_rows, :], preferred_element_type=F32)
            first = c * (CHUNK // GROUP)
            keys_t = jnp.concatenate([kt[first + n] for n in range(CHUNK // GROUP)], axis=1)
            dqt[...] += jnp.dot(keys_t, ds, preferred_element_type=F32)
            return carry

        lax.fori_loop(0, count, grads, 0)
        dq_pair = dqt[...].T * SCALE
        for n in range(2):
            g = q_group[2 * i + n]
            slot, half = lax.div(g, 8), lax.rem(g, 2)
            row = pl.multiple_of(half * GROUP, GROUP)
            part = dq_pair[GROUP * n : GROUP * n + GROUP]
            dq[slot, pl.ds(row, GROUP), :] = part[:, 0:128].astype(BF16)
            both = part[:, 128:256]
            dq_rope[2 * slot + half] = both + swap_halves(both)

    for slot in range(4):
        dq[slot, 256:384, :] = jnp.where(low, dq_rope[2 * slot], dq_rope[2 * slot + 1]).astype(BF16)

    @pl.loop(0, GROUPS)
    def _(p):
        g = held[p]
        block, row = lax.div(g, 2), pl.multiple_of(lax.rem(g, 2) * GROUP, GROUP)
        rows = pl.ds(pl.multiple_of(p * GROUP, GROUP), GROUP)
        dkv[block, pl.ds(row, GROUP), :] = (dkc[rows, 0:128] * SCALE).astype(BF16)
        dkv[block, pl.ds(256 + row, GROUP), :] = dvc[rows, :].astype(BF16)
        dk_rope[g] = dkc[rows, 128:256] * SCALE

    @pl.loop(0, BLOCKS)
    def _(block):
        dkv[block, 512:640, :] = jnp.where(low, dk_rope[2 * block], dk_rope[2 * block + 1]).astype(BF16)


def attention(order, kv, qd):
    vmem = pl.BlockSpec(memory_space=pltpu.VMEM)
    seq = GROUPS * GROUP
    return pl.pallas_call(
        attention_kernel,
        name="attention",
        out_shape=(
            jax.ShapeDtypeStruct((BLOCKS, ROWS, 128), BF16),
            jax.ShapeDtypeStruct((4, DQ_ROWS, 128), BF16),
        ),
        in_specs=[
            pl.BlockSpec(memory_space=pltpu.SMEM),
            pl.BlockSpec(memory_space=pl.ANY),
            vmem,
        ],
        out_specs=(vmem, vmem),
        scratch_shapes=[
            pltpu.SMEM((GROUPS,), jnp.int32),
            pltpu.SMEM((16,), jnp.int32),
            pltpu.SMEM((16,), jnp.int32),
            pltpu.VMEM((seq, 256), BF16),
            pltpu.VMEM((GROUPS, 256, GROUP), BF16),
            pltpu.VMEM((seq, 128), BF16),
            pltpu.VMEM((seq, 128), BF16),
            pltpu.VMEM((1024, 256), BF16),
            pltpu.VMEM((4, 256, PAIR), BF16),
            pltpu.VMEM((1024, 128), BF16),
            pltpu.VMEM((4, 128, PAIR), BF16),
            pltpu.VMEM((seq, PAIR), F32),
            pltpu.VMEM((seq, PAIR), F32),
            pltpu.VMEM((seq, 256), F32),
            pltpu.VMEM((seq, 128), F32),
            pltpu.VMEM((256, PAIR), F32),
            pltpu.VMEM((8, GROUP, 128), F32),
            pltpu.VMEM((GROUPS, GROUP, 128), F32),
            pltpu.SemaphoreType.DMA((3, GROUPS)),
        ],
        compiler_params=pltpu.CompilerParams(vmem_limit_bytes=48 * MIB),
    )(order, kv, qd)


def reduce_kernel(
    heads, dkv, dq, lat, uk, uv, gqn, gqr, gl, gr, guk, guv,
    rc, sy, ry, sx, rx, rdq, sl, rl, ag, gp, gc, sgy, rgy, sgx, rgx,
    send_c, recv_c, send_q, recv_q, send_y, recv_y, send_x, recv_x, send_l, recv_l, send_a, recv_a,
    send_g, recv_g, send_gx, recv_gx,
):
    me = lax.axis_index("ctx")
    head = lax.axis_index("head")
    x, quarter, y, core, y_mate, core_mate = place_of(me)
    piece = TOKENS // heads
    barrier = pltpu.get_barrier_semaphore()
    for o in (1, 2, 3):
        pl.semaphore_signal(
            barrier, inc=1, device_id={"ctx": 4 * lax.rem(x + o, 4) + quarter}, device_id_type=MESH
        )
    for mate in (y_mate, core_mate):
        pl.semaphore_signal(barrier, inc=1, device_id={"ctx": mate}, device_id_type=MESH)
    for o in range(1, heads):
        pl.semaphore_signal(
            barrier, inc=1, device_id={"head": lax.rem(head + o, heads)}, device_id_type=MESH
        )
    pl.semaphore_wait(barrier, 5 + heads - 1)

    started = []

    def send(*args):
        copy = remote(*args)
        copy.start()
        started.append(copy)

    turn = (1, 3, 2, 0)
    for far in (1, 0):
        for o in turn:
            other = lax.rem(x + o, 4)
            side = (1 - y) if far else y
            slot = 4 * (1 - far) + other
            send(
                dkv.at[4 * other + 2 * side + (1 - core)], rc.at[slot],
                send_c.at[slot], recv_c.at[slot], core_mate,
            )
    for o in (1, 3, 2):
        other = lax.rem(x + o, 4)
        send(dq.at[other], rdq.at[x], send_q.at[o - 1], recv_q.at[x], 4 * other + quarter)
    rdq[x] = dq[x]

    def from_core(slot):
        remote(rc.at[slot], rc.at[slot], send_c.at[0], recv_c.at[slot], core_mate).wait_recv()

    for o in turn:
        other = lax.rem(x + o, 4)
        from_core(other)
        sy[other] = (
            dkv[4 * other + 2 * (1 - y) + core].astype(F32) + rc[other].astype(F32)
        ).astype(BF16)
        send(sy.at[other], ry.at[other], send_y.at[other], recv_y.at[other], y_mate)
    for o in turn:
        other = lax.rem(x + o, 4)
        from_core(4 + other)
        near = dkv[4 * other + 2 * y + core].astype(F32) + rc[4 + other].astype(F32)
        remote(ry.at[other], ry.at[other], send_c.at[0], recv_y.at[other], y_mate).wait_recv()
        full = (near + ry[other].astype(F32)).astype(BF16)
        if o:
            sx[other] = full
            send(sx.at[other], rx.at[x], send_x.at[o - 1], recv_x.at[x], 4 * other + quarter)
        else:
            rx[x] = full

    low = low_lanes(128)
    for o in (1, 3, 2):
        other = lax.rem(x + o, 4)
        remote(rdq.at[other], rdq.at[other], send_c.at[0], recv_q.at[other], y_mate).wait_recv()
    for h in range(4):
        gqn[:, 128 * h : 128 * h + 128] = rdq[h, 0:256, :]
    for two in range(2):
        a = rdq[2 * two, 256:384, :].astype(F32)
        b = rdq[2 * two + 1, 256:384, :].astype(F32)
        cols = slice(128 * two, 128 * two + 128)
        gqr[0:128, cols] = jnp.where(low, a, swap_halves(b)).astype(BF16)
        gqr[128:256, cols] = jnp.where(low, swap_halves(a), b).astype(BF16)

    for o in (1, 3, 2):
        other = lax.rem(x + o, 4)
        remote(rx.at[other], rx.at[other], send_c.at[0], recv_x.at[other], y_mate).wait_recv()
    dkeys = jnp.concatenate([rx[h, 0:256, :] for h in range(4)], axis=1)
    dvalues = jnp.concatenate([rx[h, 256:512, :] for h in range(4)], axis=1)
    part = lax.dot_general(dkeys, uk[...], NT, preferred_element_type=F32)
    part = part + lax.dot_general(dvalues, uv[...], NT, preferred_element_type=F32)
    rope = rx[0, 512:640, :].astype(F32)
    for h in range(1, 4):
        rope = rope + rx[h, 512:640, :].astype(F32)
    half = piece // 2
    for p in range(heads):
        sl[p, :, 0:512] = part[piece * p : piece * p + piece].astype(BF16)
        sl[p, 0:half, 512:640] = rope[half * p : half * p + half].astype(BF16)
        sl[p, half:piece, 512:640] = jnp.zeros((piece - half, 128), BF16)

    def send_head(src, dst, send_sem, recv_sem, to):
        copy = pltpu.make_async_remote_copy(
            src_ref=src,
            dst_ref=dst,
            send_sem=send_sem,
            recv_sem=recv_sem,
            device_id={"head": to},
            device_id_type=MESH,
        )
        copy.start()
        started.append(copy)

    for o in range(1, heads):
        to = lax.rem(head + o, heads)
        send_head(sl.at[to], rl.at[head], send_l.at[o], recv_l.at[head], to)
    rl[head] = sl[head]

    weight_keys = lax.dot_general(lat[...], dkeys, TN, preferred_element_type=F32).astype(BF16)
    weight_values = lax.dot_general(lat[...], dvalues, TN, preferred_element_type=F32).astype(BF16)
    for cc in range(2):
        for yy in range(2):
            for xx in range(4):
                row = 32 * (4 * xx + 2 * yy + cc)
                gp[cc, yy, xx, :, 0:512] = weight_keys[row : row + 32]
                gp[cc, yy, xx, :, 512:1024] = weight_values[row : row + 32]
    send(gp.at[1 - core], gc, send_g.at[0], recv_g.at[0], core_mate)

    for o in range(1, heads):
        source = lax.rem(head + o, heads)
        remote(rl.at[source], rl.at[source], send_c.at[0], recv_l.at[source], y_mate).wait_recv()
    summed = rl[0].astype(F32)
    for p in range(1, heads):
        summed = summed + rl[p].astype(F32)
    ag[head] = summed.astype(BF16)
    for o in range(1, heads):
        to = lax.rem(head + o, heads)
        send_head(ag.at[head], ag.at[head], send_a.at[o], recv_a.at[head], to)

    remote(gc, gc, send_c.at[0], recv_g.at[0], core_mate).wait_recv()
    sgy[...] = (gp[core, 1 - y].astype(F32) + gc[1 - y].astype(F32)).astype(BF16)
    send(sgy, rgy, send_g.at[1], recv_g.at[1], y_mate)
    near_g = gp[core, y].astype(F32) + gc[y].astype(F32)
    remote(rgy, rgy, send_c.at[0], recv_g.at[1], y_mate).wait_recv()
    sgx[...] = (near_g + rgy[...].astype(F32)).astype(BF16)
    for o in (1, 3, 2):
        other = lax.rem(x + o, 4)
        send(sgx.at[other], rgx.at[x], send_gx.at[o - 1], recv_gx.at[x], 4 * other + quarter)
    rgx[x] = sgx[x]
    for o in (1, 3, 2):
        other = lax.rem(x + o, 4)
        remote(rgx.at[other], rgx.at[other], send_c.at[0], recv_gx.at[other], y_mate).wait_recv()
    weights = rgx[0].astype(F32)
    for h in range(1, 4):
        weights = weights + rgx[h].astype(F32)
    guk[...] = weights[:, 0:512]
    guv[...] = weights[:, 512:1024]

    for o in range(1, heads):
        source = lax.rem(head + o, heads)
        remote(ag.at[source], ag.at[source], send_c.at[0], recv_a.at[source], y_mate).wait_recv()
    for p in range(heads):
        gl[piece * p : piece * p + piece, :] = ag[p, :, 0:512].astype(F32)
        packed = ag[p, 0:half, 512:640].astype(F32)
        gr[half * p : half * p + half, :] = packed[:, 0:64]
        gr[128 + half * p : 128 + half * p + half, :] = swap_halves(packed)[:, 0:64]
    for copy in started:
        copy.wait_send()


def reduce(heads, dkv, dq, lat, uk, uv):
    vmem = pl.BlockSpec(memory_space=pltpu.VMEM)
    piece = TOKENS // heads
    dma = pltpu.SemaphoreType.DMA
    return pl.pallas_call(
        functools.partial(reduce_kernel, heads),
        name="reduce",
        out_shape=(
            jax.ShapeDtypeStruct((TOKENS, 512), BF16),
            jax.ShapeDtypeStruct((TOKENS, 256), BF16),
            jax.ShapeDtypeStruct((TOKENS, 512), F32),
            jax.ShapeDtypeStruct((TOKENS, 64), F32),
            jax.ShapeDtypeStruct((32, 512), F32),
            jax.ShapeDtypeStruct((32, 512), F32),
        ),
        in_specs=[vmem] * 5,
        out_specs=(vmem,) * 6,
        scratch_shapes=[
            pltpu.VMEM((8, ROWS, 128), BF16),
            pltpu.VMEM((4, ROWS, 128), BF16),
            pltpu.VMEM((4, ROWS, 128), BF16),
            pltpu.VMEM((4, ROWS, 128), BF16),
            pltpu.VMEM((4, ROWS, 128), BF16),
            pltpu.VMEM((4, DQ_ROWS, 128), BF16),
            pltpu.VMEM((heads, piece, 640), BF16),
            pltpu.VMEM((heads, piece, 640), BF16),
            pltpu.VMEM((heads, piece, 640), BF16),
            pltpu.VMEM((2, 2, 4, 32, 1024), BF16),
            pltpu.VMEM((2, 4, 32, 1024), BF16),
            pltpu.VMEM((4, 32, 1024), BF16),
            pltpu.VMEM((4, 32, 1024), BF16),
            pltpu.VMEM((4, 32, 1024), BF16),
            pltpu.VMEM((4, 32, 1024), BF16),
            dma((8,)), dma((8,)),
            dma((3,)), dma((4,)),
            dma((4,)), dma((4,)),
            dma((3,)), dma((4,)),
            dma((heads,)), dma((heads,)),
            dma((heads,)), dma((heads,)),
            dma((2,)), dma((2,)),
            dma((3,)), dma((4,)),
        ],
        compiler_params=pltpu.CompilerParams(
            collective_id=1, has_side_effects=True, vmem_limit_bytes=40 * MIB
        ),
    )(dkv, dq, lat, uk, uv)


def per_device(q_nope, q_rope, latent, rope_keys, out_grad, up_keys, up_values, group_order):
    kv, qd = exchange(q_nope, q_rope, out_grad, latent, rope_keys, up_keys, up_values)
    dkv, dq = attention(group_order, kv, qd)
    return reduce(lax.axis_size("head"), dkv, dq, latent, up_keys, up_values)


def solution(mesh):
    in_specs = (
        P("ctx", "head"),
        P("ctx", "head"),
        P("ctx", None),
        P("ctx", None),
        P("ctx", "head"),
        P(None, "head"),
        P(None, "head"),
        P(),
    )
    out_specs = (
        P("ctx", "head"),
        P("ctx", "head"),
        P("ctx", None),
        P("ctx", None),
        P("ctx", "head"),
        P("ctx", "head"),
    )
    return jax.shard_map(
        per_device, mesh=mesh, in_specs=in_specs, out_specs=out_specs, check_vma=False
    )
```

time: 754 us -> 108 us (0.14)
  waiting for transfers between devices: 461 us -> 0 us
  local copies, waits for them, and re-layouts: 116 us -> 13 us
  matrix products: 102 us -> 0 us
  Pallas kernels: 0 us -> 92.9 us
  other arithmetic: 23.3 us -> 0 us
  blocking collectives: 22.9 us -> 0 us
  between operations: 14.4 us -> 0.71 us
  loops' own time: 11.6 us -> 0 us
    reduce_scatter x2 -> x0, waiting for transfers between devices: 239 us -> none  [the longest x1 174 us: per_device(): lax.psum_scatter(pair_stack.reshape(seq_len, pair_cols), 'ctx', scatter_d...]
    unnamed x8 -> x0, waiting for transfers between devices: 126 us -> none
    dot_general x94 -> x0, matrix products: 102 us -> none  [the longest x16 25.4 us: block_scores(): jnp.einsum('thr,kr->htk', query_rope, rope_rows, preferred_element_type=j...]
    pallas_call x0 -> x3, Pallas kernels: none -> 92.9 us  [the longest x1 47.9 us: reduce(): pl.pallas_call(functools.partial(reduce_kernel, heads), name='reduce', ou...]
    psum x1 -> x0, waiting for transfers between devices: 80 us -> none  [per_device(): grad_latent, grad_rope = lax.psum((latent_part, rope_part), 'head')]
    dynamic_update_slice x32 -> x0, local copies, waits for them, and re-layouts: 58.2 us -> none  [per_device(): lax.scan(grad_visit, (start_nope, start_rope), jnp.arange(block_count, dt...]
    dynamic_slice x32 -> x0, local copies, waits for them, and re-layouts: 29.8 us -> none  [the longest x16 20.5 us: fetch(): lax.dynamic_slice_in_dim(values_all, start, count, 0)]
    all_gather x1 -> x0, blocking collectives: 22.9 us -> none  [per_device(): lax.all_gather(rope_keys, 'ctx', axis=0, tiled=True)]
  transfers between devices with their start and end apart: 6 -> 0, of which waited for: 6 -> 0; matrix products, arithmetic and copies ran while one was open for 2% -> 0% of each run, Pallas kernels for 0% -> 0%
where the time goes in v1:
time: 108 us; the launch traced here: 107 us
  Pallas kernels  92.9 us (86%)
  local copies, waits for them, and re-layouts  13 us (12%)
    pallas_call x1, Pallas kernels, reduce(): pl.pallas_call(functools.partial(reduce_kernel, heads), name='reduce', ou...  47.9 us
    pallas_call x1, Pallas kernels, attention(): pl.pallas_call(attention_kernel, name='attention', out_shape=(jax.ShapeDt...  24.2 us
    pallas_call x1, Pallas kernels, exchange(): pl.pallas_call(exchange_kernel, name='exchange', out_shape=(jax.ShapeDtyp...  20.9 us
    unnamed x28, local copies, waits for them, and re-layouts  12.3 us

profile of v1, /device:TPU:0, one launch (start us, length us, event | category | flops | bytes accessed | tf_op | source)
XLA Modules:
  0.0 106.6 jit_solution(4920790829298379754)
XLA Ops:
  0.6 0.9 copy.14.rope
  1.5 0.0 copy-start.1
  1.5 1.0 copy-done.1
  2.6 0.0 copy-start.3
  2.6 1.0 copy-done.3
  3.6 0.0 copy-start.5
  3.6 0.9 copy-done.5
  4.5 0.0 copy-start.7
  4.5 0.9 copy-done.7
  5.5 0.0 copy-start.8
  5.5 0.9 copy-done.8
  6.4 0.0 copy-start.9
  6.5 0.9 copy-done.9
  7.4 0.0 copy-start.2
  7.4 0.0 copy-start.4
  7.4 0.0 copy-start.6
  7.4 20.9 %exchange.1 = (bf16[16,640,128]{2,1,0:T(8,128)(2,1)S(1)}, bf16[4,640,128]{2,1,0:T(8,128)(2,1)S(1)}) custom-call(bf16[256,512]{1,0:T(8,128)(2,1)S(1)} %copy-done.7, bf16[256,256]{1,0:T(8,128)(2,1)S(1)} %copy-done.9, bf16[256,512]{1,0:T(8,128)(2,1)S(1)} %copy-done.8, bf16[256,512]{1,0:T(8,128)(2,1)S(1)} %copy-done.5, bf16[256,64]{1,0:T(8,128)(2,1)S(1)} %copy.14.rope, ...), custom_call_target="tpu_custom_call" | custom-call | tf_op jit(solution)/shard_map/exchange/pallas_call | solution.py:155
  28.3 0.0 copy-start
  28.3 1.5 %copy-done = bf16[16,640,128]{2,1,0:T(8,128)(2,1)} copy-done((bf16[16,640,128]{2,1,0:T(8,128)(2,1)}, bf16[16,640,128]{2,1,0:T(8,128)(2,1)S(1)}, u32[]{:S(2)}) %copy-start) | copy-done | bytes 2621464
  29.8 0.0 copy-start.10
  29.8 0.7 copy-done.10
  30.5 24.2 %attention.1 = (bf16[16,640,128]{2,1,0:T(8,128)(2,1)S(1)}, bf16[4,384,128]{2,1,0:T(8,128)(2,1)S(1)}) custom-call(s32[32]{0:T(128)S(1)} %copy-done.10, bf16[16,640,128]{2,1,0:T(8,128)(2,1)} %copy-done, bf16[4,640,128]{2,1,0:T(8,128)(2,1)S(1)} %get-tuple-element.11.qd), custom_call_target="tpu_custom_call" | custom-call | tf_op jit(solution)/shard_map/attention/pallas_call | solution.py:343
  54.6 0.0 copy-done.2
  54.6 0.0 copy-done.4
  54.6 0.0 copy-done.6
  54.6 47.9 %reduce.1 = (bf16[256,512]{1,0:T(8,128)(2,1)S(1)}, bf16[256,256]{1,0:T(8,128)(2,1)S(1)}, f32[256,512]{1,0:T(8,128)S(1)}, f32[256,64]{1,0:T(8,128)S(1)}, f32[32,512]{1,0:T(8,128)S(1)}, /*index=5*/f32[32,512]{1,0:T(8,128)S(1)}) custom-call(bf16[16,640,128]{2,1,0:T(8,128)(2,1)S(1)} %get-tuple-element.12.dkv, bf16[4,384,128]{2,1,0:T(8,128)(2,1)S(1)} %get-tuple-element.13.dq, ...), custom_call_target="tpu_custom_call" | custom-call | tf_op jit(solution)/shard_map/reduce/pallas_call | solution.py:550
  102.5 0.7 copy.15
  103.2 0.7 copy.21
  103.9 0.7 copy.22
  104.6 0.8 copy.23
  105.4 0.6 copy.24
  106.0 0.6 copy.25
Async XLA Ops:
  1.5 1.0 copy-start.1
  2.6 1.0 copy-start.3
  3.6 0.9 copy-start.5
  4.5 0.9 copy-start.7
  5.5 0.9 copy-start.8
  6.4 0.9 copy-start.9
  7.4 47.3 %copy-start.2 = (bf16[512,512]{1,0:T(8,128)(2,1)S(1)}, bf16[512,512]{1,0:T(8,128)(2,1)}, u32[]{:S(2)}) copy-start(bf16[512,512]{1,0:T(8,128)(2,1)} %uk.3) | copy-start | bytes 1572868
  7.4 47.3 %copy-start.4 = (bf16[512,512]{1,0:T(8,128)(2,1)S(1)}, bf16[512,512]{1,0:T(8,128)(2,1)}, u32[]{:S(2)}) copy-start(bf16[512,512]{1,0:T(8,128)(2,1)} %uv.3) | copy-start | bytes 1572868
  7.4 47.3 %copy-start.6 = (bf16[256,512]{1,0:T(8,128)(2,1)S(1)}, bf16[256,512]{1,0:T(8,128)(2,1)}, u32[]{:S(2)}) copy-start(bf16[256,512]{1,0:T(8,128)(2,1)} %lat.3) | copy-start | bytes 786436
  28.3 1.5 %copy-start = (bf16[16,640,128]{2,1,0:T(8,128)(2,1)}, bf16[16,640,128]{2,1,0:T(8,128)(2,1)S(1)}, u32[]{:S(2)}) copy-start(bf16[16,640,128]{2,1,0:T(8,128)(2,1)S(1)} %get-tuple-element.10.kv) | copy-start | bytes 7864324
  29.8 0.7 copy-start.10

commit v2 on v0

v2 whole, which is shorter than its diff:
```python
import functools
import math

import jax
import jax.numpy as jnp
from jax import lax
from jax.experimental import pallas as pl
from jax.experimental.pallas import tpu as pltpu
from jax.sharding import PartitionSpec as P

MESH = pl.DeviceIdType.MESH
F32 = jnp.float32
BF16 = jnp.bfloat16

SCALE = (128 + 64) ** (-0.5)
EXP2_SCALE = SCALE * math.log2(math.e)
NEG_LARGE = -1e30

GROUP = 128
GROUPS = 32
BLOCKS = 16
TOKENS = 256
ROWS = 640
DQ_ROWS = 384
MIB = 1024 * 1024

NT = (((1,), (1,)), ((), ()))
TN = (((0,), (0,)), ((), ()))


def low_lanes(rows):
    return lax.broadcasted_iota(jnp.int32, (rows, 128), 1) < 64


def swap_halves(tile):
    return pltpu.roll(tile, 64, 1)


def place_of(me):
    x = lax.div(me, 4)
    quarter = lax.rem(me, 4)
    core = lax.rem(quarter, 2)
    y = lax.div(quarter, 2)
    y_mate = 4 * x + 2 * (1 - y) + core
    core_mate = 4 * x + 2 * y + (1 - core)
    return x, quarter, y, core, y_mate, core_mate


def remote(src, dst, send_sem, recv_sem, ctx):
    return pltpu.make_async_remote_copy(
        src_ref=src,
        dst_ref=dst,
        send_sem=send_sem,
        recv_sem=recv_sem,
        device_id={"ctx": ctx},
        device_id_type=MESH,
    )


def fused_kernel(
    heads, order, qn_in, qr_in, og_in, lat_in, rope_in, uk_in, uv_in,
    gqn, gqr, gl, gr, guk, guv,
    qn, qr, og, rope, uk, uv, skv, sq, kv, qd, lats,
    rm, kt, qm, qct, doct, s_all, dp_all, tops, stats, dqt,
    dkv, rc, sy, ry, rx, sdq, rdq, wsum, gp, gc, sgy, rgy, sgx, rgx, sl, rl, ag,
    load_sem, s_kvx, s_kvy, s_kvc, r_kv, s_q, r_q, s_lat, r_lat,
    s_c, r_c, s_y, r_y, s_x, r_x, s_dq, r_dq, s_g, r_g, s_gx, r_gx, s_l, r_l, s_a, r_a,
):
    me = lax.axis_index("ctx")
    head = lax.axis_index("head")
    x, quarter, y, core, y_mate, core_mate = place_of(me)
    piece = TOKENS // heads

    def at_x(o):
        return lax.rem(x + o, 4)

    loads = [
        pltpu.make_async_copy(src, dst, load_sem.at[n])
        for n, (src, dst) in enumerate(
            (
                (lat_in, lats.at[x]), (uk_in, uk), (uv_in, uv), (rope_in, rope),
                (qn_in, qn), (qr_in, qr), (og_in, og),
            )
        )
    ]
    for copy in loads:
        copy.start()

    barrier = pltpu.get_barrier_semaphore()
    for o in (1, 2, 3):
        pl.semaphore_signal(
            barrier, inc=1, device_id={"ctx": 4 * at_x(o) + quarter}, device_id_type=MESH
        )
    for mate in (y_mate, core_mate):
        pl.semaphore_signal(barrier, inc=1, device_id={"ctx": mate}, device_id_type=MESH)
    for o in range(1, heads):
        pl.semaphore_signal(
            barrier, inc=1, device_id={"head": lax.rem(head + o, heads)}, device_id_type=MESH
        )

    started = []

    def send(*args):
        copy = remote(*args)
        copy.start()
        started.append(copy)

    def wait_recv(ref, sem):
        remote(ref, ref, s_c.at[0], sem, core_mate).wait_recv()

    for copy in loads[0:4]:
        copy.wait()
    latent = lats[x]
    keys = jnp.dot(latent, uk[...], preferred_element_type=F32).astype(BF16)
    values = jnp.dot(latent, uv[...], preferred_element_type=F32).astype(BF16)
    rope_t = rope[...].astype(F32)
    packed_rope = jnp.concatenate([rope_t[:, 0:128], rope_t[:, 128:256]], axis=0).T.astype(BF16)
    for h in range(4):
        skv[h, 0:256, :] = keys[:, 128 * h : 128 * h + 128]
        skv[h, 256:512, :] = values[:, 128 * h : 128 * h + 128]
        skv[h, 512:640, :] = packed_rope
    pl.semaphore_wait(barrier, 5 + heads - 1)

    def send_kv(o):
        send(skv.at[at_x(o)], kv.at[me], s_kvx.at[o - 1], r_kv.at[me], 4 * at_x(o) + quarter)

    def send_q(o):
        send(sq.at[at_x(o)], qd.at[x], s_q.at[o - 1], r_q.at[x], 4 * at_x(o) + quarter)

    send_kv(1)
    send_kv(3)
    send(skv.at[x], kv.at[me], s_kvy.at[0], r_kv.at[me], y_mate)
    send(skv.at[x], kv.at[me], s_kvc.at[0], r_kv.at[me], core_mate)
    low = low_lanes(128)
    for copy in loads[4:7]:
        copy.wait()
    for h in range(4):
        sq[h, 0:256, :] = qn[:, 128 * h : 128 * h + 128]
        sq[h, 256:512, :] = og[:, 128 * h : 128 * h + 128]
        tile = qr[:, 128 * (h // 2) : 128 * (h // 2) + 128].astype(F32)
        top, bottom = tile[0:128], tile[128:256]
        if h % 2 == 0:
            packed = jnp.where(low, top, swap_halves(bottom))
        else:
            packed = jnp.where(low, swap_halves(top), bottom)
        sq[h, 512:640, :] = packed.astype(BF16)
    send_q(1)
    send_q(3)
    send_kv(2)
    send_q(2)
    kv[me] = skv[x]
    qd[x] = sq[x]

    lane = lax.broadcasted_iota(jnp.int32, (128, 128), 1)

    def prepare_keys(block):
        packed = kv[block, 512:640, :].astype(F32)
        for half in range(2):
            place = order[2 * block + half]
            hidden = jnp.where(lane < 64 + place, NEG_LARGE, 0.0)
            hidden = jnp.where(lane < 96, hidden, 0.0)
            rows = packed if half == 0 else swap_halves(packed)
            rm[block, 128 * half : 128 * half + 128, :] = jnp.where(low, rows, hidden).astype(BF16)
        kt[block, 0:128, :] = kv[block, 0:256, :].T
        kt[block, 128:256, :] = rm[block].T

    def prepare_queries(slot):
        packed = qd[slot, 512:640, :].astype(F32)
        for half in range(2):
            place = order[2 * (4 * slot + quarter) + half]
            chosen = jnp.where(lane == 64 + place, 1.0, 0.0)
            rows = packed if half == 0 else swap_halves(packed)
            qm[slot, 128 * half : 128 * half + 128, :] = jnp.where(low, rows, chosen).astype(BF16)
        qct[slot, 0:128, :] = qd[slot, 0:256, :].T
        qct[slot, 128:256, :] = qm[slot].T
        doct[slot] = qd[slot, 256:512, :].T
        tops[slot] = jnp.full((8, 256), NEG_LARGE, F32)

    def scores(key_x, query_x):
        top = tops[query_x]
        for b in range(4):
            block = 4 * key_x + lax.rem(quarter + b, 4)
            keys_in = jnp.concatenate([kv[block, 0:256, :], rm[block]], axis=1)
            s = jnp.dot(keys_in, qct[query_x], preferred_element_type=F32)
            if b == 0:
                rows = lax.broadcasted_iota(jnp.int32, (256, 256), 0)
                columns = lax.broadcasted_iota(jnp.int32, (256, 256), 1)
                limit = jnp.where(key_x == query_x, 0, 1024)
                same = (rows < 128) == (columns < 128)
                s = jnp.where(same & (rows > columns + limit), NEG_LARGE, s)
            s_all[query_x, block] = s
            top = jnp.maximum(top, jnp.max(s.reshape(32, 8, 256), axis=0))
            dp_all[query_x, block] = jnp.dot(
                kv[block, 256:512, :], doct[query_x], preferred_element_type=F32
            )
        tops[query_x] = top

    def take_x(o, n):
        block = 4 * at_x(o) + quarter
        wait_recv(kv.at[block], r_kv.at[block])
        send(kv.at[block], kv.at[block], s_kvy.at[n], r_kv.at[block], y_mate)
        send(kv.at[block], kv.at[block], s_kvc.at[n], r_kv.at[block], core_mate)

    def take_y(o, n):
        block = 4 * at_x(o) + 2 * (1 - y) + core
        wait_recv(kv.at[block], r_kv.at[block])
        send(kv.at[block], kv.at[block], s_kvc.at[n], r_kv.at[block], core_mate)

    def take_set(o, n):
        take_y(o, n)
        for side in range(2):
            block = 4 * at_x(o) + 2 * side + (1 - core)
            wait_recv(kv.at[block], r_kv.at[block])

        @pl.loop(0, 4)
        def _(b):
            prepare_keys(4 * at_x(o) + b)

    def take_queries(o):
        wait_recv(qd.at[at_x(o)], r_q.at[at_x(o)])
        prepare_queries(at_x(o))

    prepare_queries(x)
    take_x(1, 1)
    take_x(3, 2)
    take_set(0, 4)
    scores(x, x)
    take_set(1, 5)
    scores(at_x(1), x)
    take_queries(1)

    @pl.loop(0, 2)
    def _(n):
        scores(at_x(n), at_x(1))

    take_x(2, 3)
    take_queries(3)

    @pl.loop(0, 2)
    def _(n):
        scores(at_x(n), at_x(3))

    take_set(3, 6)

    @pl.loop(0, 3)
    def _(n):
        scores(at_x(3), at_x(n + lax.div(n, 2)))

    take_queries(2)
    for o in (1, 3, 2):
        send(lats.at[x], lats.at[x], s_lat.at[o - 1], r_lat.at[x], 4 * at_x(o) + quarter)

    @pl.loop(0, 3)
    def _(n):
        scores(at_x(n + lax.div(n, 2)), at_x(2))

    take_set(2, 7)

    @pl.loop(0, 4)
    def _(n):
        scores(at_x(2), at_x(n))

    @pl.loop(0, 4)
    def _(i):
        top = jnp.max(tops[i], axis=0, keepdims=True) * EXP2_SCALE

        @pl.loop(0, 4, init_carry=(jnp.zeros((8, 256), F32), jnp.zeros((8, 256), F32)))
        def sums(n, carry):
            total, weighted = carry
            for b in range(4):
                block = 4 * n + b
                p = jnp.exp2(s_all[i, block] * EXP2_SCALE - top)
                s_all[i, block] = p
                total = total + jnp.sum(p.reshape(32, 8, 256), axis=0)
                weighted = weighted + jnp.sum((p * dp_all[i, block]).reshape(32, 8, 256), axis=0)
            return total, weighted

        inverse = 1.0 / jnp.sum(sums[0], axis=0, keepdims=True)
        stats[0, i] = inverse
        stats[1, i] = jnp.sum(sums[1], axis=0, keepdims=True) * inverse
        dqt[i] = jnp.zeros((256, 256), F32)

    def grads(first, second):
        blocks = (first, second)
        dk = [jnp.zeros((256, 256), F32)] * 2
        dv = [jnp.zeros((256, 128), F32)] * 2
        for i in range(4):
            inverse, delta = stats[0, i], stats[1, i]
            queries = jnp.concatenate([qd[i, 0:256, :], qm[i]], axis=1)
            ds = []
            for n, block in enumerate(blocks):
                attn = s_all[i, block] * inverse
                ds.append((attn * (dp_all[i, block] - delta)).astype(BF16))
                dv[n] = dv[n] + jnp.dot(
                    attn.astype(BF16), qd[i, 256:512, :], preferred_element_type=F32
                )
                dk[n] = dk[n] + jnp.dot(ds[n], queries, preferred_element_type=F32)
            keys_t = jnp.concatenate([kt[first], kt[second]], axis=1)
            dqt[i] += jnp.dot(keys_t, jnp.concatenate(ds, axis=0), preferred_element_type=F32)
        for n, block in enumerate(blocks):
            scaled = dk[n] * SCALE
            dkv[block, 0:256, :] = scaled[:, 0:128].astype(BF16)
            dkv[block, 256:512, :] = dv[n].astype(BF16)
            tail = scaled[:, 128:256]
            dkv[block, 512:640, :] = jnp.where(low, tail[0:128], swap_halves(tail[128:256])).astype(
                BF16
            )

    def to_core(slot, block):
        return remote(dkv.at[block], rc.at[slot], s_c.at[slot], r_c.at[slot], core_mate)

    def to_y(other):
        return remote(sy.at[other], ry.at[other], s_y.at[other], r_y.at[other], y_mate)

    def pass_far(other):
        wait_recv(rc.at[other], r_c.at[other])
        mine = dkv[4 * other + 2 * (1 - y) + core].astype(F32)
        sy[other] = (mine + rc[other].astype(F32)).astype(BF16)
        to_y(other).start()

    @pl.loop(0, 8)
    def _(n):
        near = lax.div(n, 4)
        other = at_x(1 + lax.rem(n, 4))
        side = near * y + (1 - near) * (1 - y)
        out = 4 * other + 2 * side + (1 - core)
        grads(out, 4 * other + 2 * side + core)
        to_core(4 * near + other, out).start()

        @pl.when((n > 0) & (n < 5))
        def _():
            pass_far(at_x(n))

    for i in range(4):
        whole = dqt[i].T * SCALE
        sdq[i, 0:256, :] = whole[:, 0:128].astype(BF16)
        tail = whole[:, 128:256]
        sdq[i, 256:384, :] = jnp.where(low, tail[0:128], swap_halves(tail[128:256])).astype(BF16)
    rdq[x] = sdq[x]

    for o in (1, 2, 3, 0):
        other = at_x(o)
        wait_recv(rc.at[4 + other], r_c.at[4 + other])
        block = 4 * other + 2 * y + core
        near = dkv[block].astype(F32) + rc[4 + other].astype(F32)
        wait_recv(ry.at[other], r_y.at[other])
        full = (near + ry[other].astype(F32)).astype(BF16)
        dkv[block] = full
        if o:
            send(dkv.at[block], rx.at[x], s_x.at[o - 1], r_x.at[x], 4 * other + quarter)
            wait_recv(lats.at[other], r_lat.at[other])
        else:
            rx[x] = full
        pair = jnp.concatenate([full[0:256], full[256:512]], axis=1)
        term = lax.dot_general(lats[other], pair, TN, preferred_element_type=F32)
        if o == 1:
            wsum[...] = term
        elif o:
            wsum[...] += term
        else:
            total = (wsum[...] + term).astype(BF16)
        if o == 3:
            for oo in (1, 3, 2):
                send(
                    sdq.at[at_x(oo)], rdq.at[x], s_dq.at[oo - 1], r_dq.at[x], 4 * at_x(oo) + quarter
                )

    for cc in range(2):
        for yy in range(2):
            for xx in range(4):
                row = 32 * (4 * xx + 2 * yy + cc)
                gp[cc, yy, xx] = total[row : row + 32]
    send(gp.at[1 - core], gc, s_g.at[0], r_g.at[0], core_mate)

    def latent_term(h):
        columns = pl.ds(pl.multiple_of(128 * h, 128), 128)
        term = lax.dot_general(rx[h, 0:256, :], uk[:, columns], NT, preferred_element_type=F32)
        return term + lax.dot_general(
            rx[h, 256:512, :], uv[:, columns], NT, preferred_element_type=F32
        )

    summed = latent_term(x)
    turned = rx[x, 512:640, :].astype(F32)
    for o in (3, 2, 1):
        wait_recv(rx.at[at_x(o)], r_x.at[at_x(o)])
        summed = summed + latent_term(at_x(o))
        turned = turned + rx[at_x(o), 512:640, :].astype(F32)
    half = piece // 2
    for p in range(heads):
        sl[p, :, 0:512] = summed[piece * p : piece * p + piece].astype(BF16)
        sl[p, 0:half, 512:640] = turned[half * p : half * p + half].astype(BF16)
        sl[p, half:piece, 512:640] = jnp.zeros((piece - half, 128), BF16)

    def send_head(src, dst, send_sem, recv_sem, to):
        copy = pltpu.make_async_remote_copy(
            src_ref=src,
            dst_ref=dst,
            send_sem=send_sem,
            recv_sem=recv_sem,
            device_id={"head": to},
            device_id_type=MESH,
        )
        copy.start()
        started.append(copy)

    for o in range(1, heads):
        to = lax.rem(head + o, heads)
        send_head(sl.at[to], rl.at[head], s_l.at[o], r_l.at[head], to)
    rl[head] = sl[head]

    wait_recv(gc, r_g.at[0])
    sgy[...] = (gp[core, 1 - y].astype(F32) + gc[1 - y].astype(F32)).astype(BF16)
    send(sgy, rgy, s_g.at[1], r_g.at[1], y_mate)
    near_g = gp[core, y].astype(F32) + gc[y].astype(F32)

    for o in (1, 2, 3):
        wait_recv(rdq.at[at_x(o)], r_dq.at[at_x(o)])
    for h in range(4):
        gqn[:, 128 * h : 128 * h + 128] = rdq[h, 0:256, :]
    for two in range(2):
        a = rdq[2 * two, 256:384, :].astype(F32)
        b = rdq[2 * two + 1, 256:384, :].astype(F32)
        cols = slice(128 * two, 128 * two + 128)
        gqr[0:128, cols] = jnp.where(low, a, swap_halves(b)).astype(BF16)
        gqr[128:256, cols] = jnp.where(low, swap_halves(a), b).astype(BF16)

    wait_recv(rgy, r_g.at[1])
    sgx[...] = (near_g + rgy[...].astype(F32)).astype(BF16)
    for o in (1, 3, 2):
        send(sgx.at[at_x(o)], rgx.at[x], s_gx.at[o - 1], r_gx.at[x], 4 * at_x(o) + quarter)
    rgx[x] = sgx[x]

    for o in range(1, heads):
        source = lax.rem(head + o, heads)
        wait_recv(rl.at[source], r_l.at[source])
    over_heads = rl[0].astype(F32)
    for p in range(1, heads):
        over_heads = over_heads + rl[p].astype(F32)
    ag[head] = over_heads.astype(BF16)
    for o in range(1, heads):
        to = lax.rem(head + o, heads)
        send_head(ag.at[head], ag.at[head], s_a.at[o], r_a.at[head], to)

    for o in (1, 2, 3):
        wait_recv(rgx.at[at_x(o)], r_gx.at[at_x(o)])
    for h in range(4):
        guk[:, 128 * h : 128 * h + 128] = rgx[h, :, 0:128].astype(F32)
        guv[:, 128 * h : 128 * h + 128] = rgx[h, :, 128:256].astype(F32)

    for o in range(1, heads):
        source = lax.rem(head + o, heads)
        wait_recv(ag.at[source], r_a.at[source])
    packed = []
    for p in range(heads):
        gl[piece * p : piece * p + piece, :] = ag[p, :, 0:512].astype(F32)
        packed.append(ag[p, 0:half, 512:640].astype(F32))
    turned_t = jnp.concatenate(packed, axis=0).T
    gr[:, 0:128] = turned_t[0:64]
    gr[:, 128:256] = turned_t[64:128]

    for copy in started:
        copy.wait_send()
    for other in range(4):
        to_y(other).wait_send()
        to_core(other, other).wait_send()
        to_core(4 + other, other).wait_send()


def fused(heads, order, qn, qr, og, lat, rope_t, uk, uv):
    hbm = pl.BlockSpec(memory_space=pltpu.HBM)
    vmem = pl.BlockSpec(memory_space=pltpu.VMEM)
    piece = TOKENS // heads
    dma = pltpu.SemaphoreType.DMA
    bf = lambda *shape: pltpu.VMEM(shape, BF16)
    f32 = lambda *shape: pltpu.VMEM(shape, F32)
    return pl.pallas_call(
        functools.partial(fused_kernel, heads),
        name="fused",
        out_shape=(
            jax.ShapeDtypeStruct((TOKENS, 512), BF16),
            jax.ShapeDtypeStruct((TOKENS, 256), BF16),
            jax.ShapeDtypeStruct((TOKENS, 512), F32),
            jax.ShapeDtypeStruct((64, TOKENS), F32),
            jax.ShapeDtypeStruct((32, 512), F32),
            jax.ShapeDtypeStruct((32, 512), F32),
        ),
        in_specs=[pl.BlockSpec(memory_space=pltpu.SMEM)] + [hbm] * 7,
        out_specs=(vmem,) * 6,
        scratch_shapes=[
            bf(256, 512), bf(256, 256), bf(256, 512), bf(64, 256), bf(512, 512), bf(512, 512),
            bf(4, ROWS, 128), bf(4, ROWS, 128), bf(BLOCKS, ROWS, 128), bf(4, ROWS, 128),
            bf(4, 256, 512),
            bf(BLOCKS, 256, 128), bf(BLOCKS, 256, 256), bf(4, 256, 128), bf(4, 256, 256),
            bf(4, 128, 256),
            f32(4, BLOCKS, 256, 256), f32(4, BLOCKS, 256, 256), f32(4, 8, 256), f32(2, 4, 1, 256),
            f32(4, 256, 256),
            bf(BLOCKS, ROWS, 128), bf(8, ROWS, 128), bf(4, ROWS, 128), bf(4, ROWS, 128),
            bf(4, ROWS, 128), bf(4, DQ_ROWS, 128), bf(4, DQ_ROWS, 128),
            f32(512, 256),
            bf(2, 2, 4, 32, 256), bf(2, 4, 32, 256), bf(4, 32, 256), bf(4, 32, 256),
            bf(4, 32, 256), bf(4, 32, 256),
            bf(heads, piece, 640), bf(heads, piece, 640), bf(heads, piece, 640),
            dma((7,)), dma((3,)), dma((4,)), dma((8,)), dma((BLOCKS,)), dma((3,)), dma((4,)),
            dma((3,)), dma((4,)),
            dma((8,)), dma((8,)), dma((4,)), dma((4,)), dma((3,)), dma((4,)), dma((3,)), dma((4,)),
            dma((2,)), dma((2,)), dma((3,)), dma((4,)),
            dma((heads,)), dma((heads,)), dma((heads,)), dma((heads,)),
        ],
        compiler_params=pltpu.CompilerParams(
            collective_id=0, has_side_effects=True, vmem_limit_bytes=60 * MIB
        ),
    )(order, qn, qr, og, lat, rope_t, uk, uv)


def finish_kernel(*refs):
    sources, results, sems = refs[0:6], refs[6:12], refs[12]
    copies = [
        pltpu.make_async_copy(src, dst, sems.at[n]) for n, (src, dst) in enumerate(zip(sources, results))
    ]
    for copy in copies:
        copy.start()
    for copy in copies:
        copy.wait()


def finish(*arrays):
    vmem = pl.BlockSpec(memory_space=pltpu.VMEM)
    hbm = pl.BlockSpec(memory_space=pltpu.HBM)
    return pl.pallas_call(
        finish_kernel,
        name="finish",
        out_shape=tuple(jax.ShapeDtypeStruct(a.shape, a.dtype) for a in arrays),
        in_specs=[vmem] * 6,
        out_specs=(hbm,) * 6,
        scratch_shapes=[pltpu.SemaphoreType.DMA((6,))],
    )(*arrays)


def per_device(q_nope, q_rope, latent, rope_keys, out_grad, up_keys, up_values, group_order):
    outs = fused(
        lax.axis_size("head"), group_order, q_nope, q_rope, out_grad, latent, rope_keys.T,
        up_keys, up_values,
    )
    outs = finish(*outs)
    return (outs[0], outs[1], outs[2], outs[3].T, outs[4], outs[5])


def solution(mesh):
    in_specs = (
        P("ctx", "head"),
        P("ctx", "head"),
        P("ctx", None),
        P("ctx", None),
        P("ctx", "head"),
        P(None, "head"),
        P(None, "head"),
        P(),
    )
    out_specs = (
        P("ctx", "head"),
        P("ctx", "head"),
        P("ctx", None),
        P("ctx", None),
        P("ctx", "head"),
        P("ctx", "head"),
    )
    return jax.shard_map(
        per_device, mesh=mesh, in_specs=in_specs, out_specs=out_specs, check_vma=False
    )
```

time: 754 us -> 73.8 us (0.10)
  waiting for transfers between devices: 461 us -> 0 us
  local copies, waits for them, and re-layouts: 116 us -> 0 us
  matrix products: 102 us -> 0 us
  Pallas kernels: 0 us -> 73 us
  other arithmetic: 23.3 us -> 0 us
  blocking collectives: 22.9 us -> 0 us
  between operations: 14.4 us -> 0.64 us
  loops' own time: 11.6 us -> 0 us
    reduce_scatter x2 -> x0, waiting for transfers between devices: 239 us -> none  [the longest x1 174 us: per_device(): lax.psum_scatter(pair_stack.reshape(seq_len, pair_cols), 'ctx', scatter_d...]
    unnamed x8 -> x0, waiting for transfers between devices: 126 us -> none
    dot_general x94 -> x0, matrix products: 102 us -> none  [the longest x16 25.4 us: block_scores(): jnp.einsum('thr,kr->htk', query_rope, rope_rows, preferred_element_type=j...]
    psum x1 -> x0, waiting for transfers between devices: 80 us -> none  [per_device(): grad_latent, grad_rope = lax.psum((latent_part, rope_part), 'head')]
    pallas_call x0 -> x2, Pallas kernels: none -> 73 us  [the longest x1 70.7 us: fused(): pl.pallas_call(functools.partial(fused_kernel, heads), name='fused', out_...]
    dynamic_update_slice x32 -> x0, local copies, waits for them, and re-layouts: 58.2 us -> none  [per_device(): lax.scan(grad_visit, (start_nope, start_rope), jnp.arange(block_count, dt...]
    dynamic_slice x32 -> x0, local copies, waits for them, and re-layouts: 29.8 us -> none  [the longest x16 20.5 us: fetch(): lax.dynamic_slice_in_dim(values_all, start, count, 0)]
    unnamed x27 -> x0, local copies, waits for them, and re-layouts: 25.7 us -> none
  transfers between devices with their start and end apart: 6 -> 0, of which waited for: 6 -> 0; matrix products, arithmetic and copies ran while one was open for 2% -> 0% of each run, Pallas kernels for 0% -> 0%
where the time goes in v2:
time: 73.8 us; the launch traced here: 73.7 us
  Pallas kernels  73 us (99%)
    pallas_call x1, Pallas kernels, fused(): pl.pallas_call(functools.partial(fused_kernel, heads), name='fused', out_...  70.7 us
    pallas_call x1, Pallas kernels, finish(): pl.pallas_call(finish_kernel, name='finish', out_shape=tuple((jax.ShapeDt...  2.26 us

profile of v2, /device:TPU:0, one launch (start us, length us, event | category | flops | bytes accessed | tf_op | source)
XLA Modules:
  0.0 73.7 jit_solution(9916757001354944746)
XLA Ops:
  0.6 70.7 %fused.1 = (bf16[256,512]{1,0:T(8,128)(2,1)}, bf16[256,256]{1,0:T(8,128)(2,1)}, f32[256,512]{1,0:T(8,128)}, f32[64,256]{1,0:T(8,128)}, f32[32,512]{1,0:T(8,128)}, /*index=5*/f32[32,512]{1,0:T(8,128)}) custom-call(s32[32]{0:T(128)} %order.1, bf16[256,512]{1,0:T(8,128)(2,1)} %qn_in.1, bf16[256,256]{1,0:T(8,128)(2,1)} %qr_in.1, bf16[256,512]{1,0:T(8,128)(2,1)} %og_in.1, ...), custom_call_target="tpu_custom_call" | custom-call | tf_op jit(solution)/shard_map/fused/pallas_call | solution.py:476
  71.4 2.3 %finish.1 = (bf16[256,512]{1,0:T(8,128)(2,1)}, bf16[256,256]{1,0:T(8,128)(2,1)}, f32[256,512]{1,0:T(8,128)}, f32[64,256]{1,0:T(8,128)}, f32[32,512]{1,0:T(8,128)}, /*index=5*/f32[32,512]{1,0:T(8,128)}) custom-call(bf16[256,512]{1,0:T(8,128)(2,1)} %get-tuple-element.18.refs_0_, bf16[256,256]{1,0:T(8,128)(2,1)} %get-tuple-element.19.refs_1_, ...), custom_call_target="tpu_custom_call" | custom-call | tf_op jit(solution)/shard_map/finish/pallas_call | solution.py:529

commit v3 on v2

--- a/solution.py
+++ b/solution.py
@@ -61,7 +61,7 @@
     heads, order, qn_in, qr_in, og_in, lat_in, rope_in, uk_in, uv_in,
     gqn, gqr, gl, gr, guk, guv,
     qn, qr, og, rope, uk, uv, skv, sq, kv, qd, lats,
-    rm, kt, qm, qct, doct, s_all, dp_all, tops, stats, dqt,
+    rm, kt, qm, qct, doct, s_all, dp_all, stats, dqt,
     dkv, rc, sy, ry, rx, sdq, rdq, wsum, gp, gc, sgy, rgy, sgx, rgx, sl, rl, ag,
     load_sem, s_kvx, s_kvy, s_kvc, r_kv, s_q, r_q, s_lat, r_lat,
     s_c, r_c, s_y, r_y, s_x, r_x, s_dq, r_dq, s_g, r_g, s_gx, r_gx, s_l, r_l, s_a, r_a,
@@ -69,6 +69,7 @@
     me = lax.axis_index("ctx")
     head = lax.axis_index("head")
     x, quarter, y, core, y_mate, core_mate = place_of(me)
+    z = lax.rem(head, 4)
     piece = TOKENS // heads
 
     def at_x(o):
@@ -78,8 +79,8 @@
         pltpu.make_async_copy(src, dst, load_sem.at[n])
         for n, (src, dst) in enumerate(
             (
-                (lat_in, lats.at[x]), (uk_in, uk), (uv_in, uv), (rope_in, rope),
-                (qn_in, qn), (qr_in, qr), (og_in, og),
+                *((lat_in.at[:, pl.ds(128 * k, 128)], lats.at[k, x]) for k in range(4)),
+                (uk_in, uk), (uv_in, uv), (rope_in, rope), (qn_in, qn), (qr_in, qr), (og_in, og),
             )
         )
     ]
@@ -105,34 +106,62 @@
         copy.start()
         started.append(copy)
 
+    def send_head(src, dst, send_sem, recv_sem, to):
+        copy = pltpu.make_async_remote_copy(
+            src_ref=src,
+            dst_ref=dst,
+            send_sem=send_sem,
+            recv_sem=recv_sem,
+            device_id={"head": to},
+            device_id_type=MESH,
+        )
+        copy.start()
+        started.append(copy)
+
     def wait_recv(ref, sem):
         remote(ref, ref, s_c.at[0], sem, core_mate).wait_recv()
 
-    for copy in loads[0:4]:
+    for copy in loads[0:7]:
         copy.wait()
-    latent = lats[x]
+
+    def latent_rows(block_x):
+        return jnp.concatenate([lats[k, block_x] for k in range(4)], axis=1)
+
+    latent = latent_rows(x)
     keys = jnp.dot(latent, uk[...], preferred_element_type=F32).astype(BF16)
     values = jnp.dot(latent, uv[...], preferred_element_type=F32).astype(BF16)
     rope_t = rope[...].astype(F32)
     packed_rope = jnp.concatenate([rope_t[:, 0:128], rope_t[:, 128:256]], axis=0).T.astype(BF16)
     for h in range(4):
         skv[h, 0:256, :] = keys[:, 128 * h : 128 * h + 128]
-        skv[h, 256:512, :] = values[:, 128 * h : 128 * h + 128]
-        skv[h, 512:640, :] = packed_rope
+        skv[h, 256:384, :] = packed_rope
+        skv[h, 384:640, :] = values[:, 128 * h : 128 * h + 128]
     pl.semaphore_wait(barrier, 5 + heads - 1)
 
+    parts = (pl.ds(0, 384), pl.ds(384, 256))
+
+    def send_block(ref, block, sem, n, ctx):
+        for m, rows in enumerate(parts):
+            send(
+                ref.at[rows], kv.at[block, rows], sem.at[2 * n + m], r_kv.at[2 * block + m], ctx
+            )
+
+    def wait_block(block):
+        for m, rows in enumerate(parts):
+            wait_recv(kv.at[block, rows], r_kv.at[2 * block + m])
+
     def send_kv(o):
-        send(skv.at[at_x(o)], kv.at[me], s_kvx.at[o - 1], r_kv.at[me], 4 * at_x(o) + quarter)
+        send_block(skv.at[at_x(o)], me, s_kvx, o - 1, 4 * at_x(o) + quarter)
 
     def send_q(o):
         send(sq.at[at_x(o)], qd.at[x], s_q.at[o - 1], r_q.at[x], 4 * at_x(o) + quarter)
 
     send_kv(1)
     send_kv(3)
-    send(skv.at[x], kv.at[me], s_kvy.at[0], r_kv.at[me], y_mate)
-    send(skv.at[x], kv.at[me], s_kvc.at[0], r_kv.at[me], core_mate)
+    send_block(skv.at[x], me, s_kvy, 0, y_mate)
+    send_block(skv.at[x], me, s_kvc, 0, core_mate)
     low = low_lanes(128)
-    for copy in loads[4:7]:
+    for copy in loads[7:10]:
         copy.wait()
     for h in range(4):
         sq[h, 0:256, :] = qn[:, 128 * h : 128 * h + 128]
@@ -154,7 +183,7 @@
     lane = lax.broadcasted_iota(jnp.int32, (128, 128), 1)
 
     def prepare_keys(block):
-        packed = kv[block, 512:640, :].astype(F32)
+        packed = kv[block, 256:384, :].astype(F32)
         for half in range(2):
             place = order[2 * block + half]
             hidden = jnp.where(lane < 64 + place, NEG_LARGE, 0.0)
@@ -174,118 +203,153 @@
         qct[slot, 0:128, :] = qd[slot, 0:256, :].T
         qct[slot, 128:256, :] = qm[slot].T
         doct[slot] = qd[slot, 256:512, :].T
-        tops[slot] = jnp.full((8, 256), NEG_LARGE, F32)
-
-    def scores(key_x, query_x):
-        top = tops[query_x]
-        for b in range(4):
-            block = 4 * key_x + lax.rem(quarter + b, 4)
+
+    def scores(key_x, side, query_x, diagonal=False):
+        slot = 2 * key_x + side
+        pair = [4 * key_x + 2 * side + core, 4 * key_x + 2 * side + (1 - core)]
+        raw, grown = [], []
+        for n, block in enumerate(pair):
             keys_in = jnp.concatenate([kv[block, 0:256, :], rm[block]], axis=1)
-            s = jnp.dot(keys_in, qct[query_x], preferred_element_type=F32)
-            if b == 0:
+            score = jnp.dot(keys_in, qct[query_x], preferred_element_type=F32)
+            if n == 0 and diagonal:
                 rows = lax.broadcasted_iota(jnp.int32, (256, 256), 0)
                 columns = lax.broadcasted_iota(jnp.int32, (256, 256), 1)
                 limit = jnp.where(key_x == query_x, 0, 1024)
                 same = (rows < 128) == (columns < 128)
-                s = jnp.where(same & (rows > columns + limit), NEG_LARGE, s)
-            s_all[query_x, block] = s
-            top = jnp.maximum(top, jnp.max(s.reshape(32, 8, 256), axis=0))
-            dp_all[query_x, block] = jnp.dot(
-                kv[block, 256:512, :], doct[query_x], preferred_element_type=F32
-            )
-        tops[query_x] = top
+                score = jnp.where(same & (rows > columns + limit), NEG_LARGE, score)
+            raw.append(score)
+            dp = jnp.dot(kv[block, 384:640, :], doct[query_x], preferred_element_type=F32)
+            dp_all[query_x, block] = dp
+            grown.append(dp)
+        tops = [jnp.max(score.reshape(32, 8, 256), axis=0) for score in raw]
+        top = jnp.max(jnp.maximum(tops[0], tops[1]), axis=0, keepdims=True) * EXP2_SCALE
+        total = jnp.zeros((8, 256), F32)
+        weighted = jnp.zeros((8, 256), F32)
+        for block, score, dp in zip(pair, raw, grown):
+            p = jnp.exp2(score * EXP2_SCALE - top)
+            s_all[query_x, block] = p
+            total = total + jnp.sum(p.reshape(32, 8, 256), axis=0)
+            weighted = weighted + jnp.sum((p * dp).reshape(32, 8, 256), axis=0)
+        stats[0, query_x, slot] = top
+        stats[1, query_x, slot] = jnp.sum(total, axis=0, keepdims=True)
+        stats[2, query_x, slot] = jnp.sum(weighted, axis=0, keepdims=True)
 
     def take_x(o, n):
         block = 4 * at_x(o) + quarter
-        wait_recv(kv.at[block], r_kv.at[block])
-        send(kv.at[block], kv.at[block], s_kvy.at[n], r_kv.at[block], y_mate)
-        send(kv.at[block], kv.at[block], s_kvc.at[n], r_kv.at[block], core_mate)
+        for m, rows in enumerate(parts):
+            wait_recv(kv.at[block, rows], r_kv.at[2 * block + m])
+            for sem, mate in ((s_kvy, y_mate), (s_kvc, core_mate)):
+                send(
+                    kv.at[block, rows], kv.at[block, rows], sem.at[2 * n + m],
+                    r_kv.at[2 * block + m], mate,
+                )
 
     def take_y(o, n):
         block = 4 * at_x(o) + 2 * (1 - y) + core
-        wait_recv(kv.at[block], r_kv.at[block])
-        send(kv.at[block], kv.at[block], s_kvc.at[n], r_kv.at[block], core_mate)
-
-    def take_set(o, n):
-        take_y(o, n)
-        for side in range(2):
-            block = 4 * at_x(o) + 2 * side + (1 - core)
-            wait_recv(kv.at[block], r_kv.at[block])
-
-        @pl.loop(0, 4)
-        def _(b):
-            prepare_keys(4 * at_x(o) + b)
+        wait_block(block)
+        send_block(kv.at[block], block, s_kvc, n, core_mate)
+
+    def take_core(o, side):
+        block = 4 * at_x(o) + 2 * side + (1 - core)
+        wait_block(block)
+        prepare_keys(4 * at_x(o) + 2 * side + core)
+        prepare_keys(block)
 
     def take_queries(o):
         wait_recv(qd.at[at_x(o)], r_q.at[at_x(o)])
         prepare_queries(at_x(o))
 
+    far = 1 - y
     prepare_queries(x)
+    take_core(0, y)
+    scores(x, y, x, True)
     take_x(1, 1)
     take_x(3, 2)
-    take_set(0, 4)
-    scores(x, x)
-    take_set(1, 5)
-    scores(at_x(1), x)
+    take_y(0, 4)
+    take_core(1, y)
+    scores(at_x(1), y, x)
+    take_core(3, y)
+    scores(at_x(3), y, x)
+    take_core(0, far)
+    scores(x, far, x)
     take_queries(1)
-
-    @pl.loop(0, 2)
-    def _(n):
-        scores(at_x(n), at_x(1))
-
+    take_queries(3)
+
+    for n in range(2):
+        for o in (0, 1, 3):
+            scores(at_x(o), y, at_x(1 + 2 * n), True)
+
+    take_y(1, 5)
     take_x(2, 3)
-    take_queries(3)
-
-    @pl.loop(0, 2)
-    def _(n):
-        scores(at_x(n), at_x(3))
-
-    take_set(3, 6)
-
-    @pl.loop(0, 3)
-    def _(n):
-        scores(at_x(3), at_x(n + lax.div(n, 2)))
-
+
+    for n in range(2):
+        scores(x, far, at_x(1 + 2 * n))
+
+    take_core(1, far)
+
+    for n in range(3):
+        scores(at_x(1), far, at_x(n + n // 2))
+
+    take_core(2, y)
+
+    for n in range(3):
+        scores(at_x(2), y, at_x(n + n // 2))
+
+    take_y(3, 6)
     take_queries(2)
     for o in (1, 3, 2):
-        send(lats.at[x], lats.at[x], s_lat.at[o - 1], r_lat.at[x], 4 * at_x(o) + quarter)
-
-    @pl.loop(0, 3)
-    def _(n):
-        scores(at_x(n + lax.div(n, 2)), at_x(2))
-
-    take_set(2, 7)
-
-    @pl.loop(0, 4)
-    def _(n):
-        scores(at_x(2), at_x(n))
-
-    @pl.loop(0, 4)
-    def _(i):
-        top = jnp.max(tops[i], axis=0, keepdims=True) * EXP2_SCALE
-
-        @pl.loop(0, 4, init_carry=(jnp.zeros((8, 256), F32), jnp.zeros((8, 256), F32)))
-        def sums(n, carry):
-            total, weighted = carry
-            for b in range(4):
-                block = 4 * n + b
-                p = jnp.exp2(s_all[i, block] * EXP2_SCALE - top)
-                s_all[i, block] = p
-                total = total + jnp.sum(p.reshape(32, 8, 256), axis=0)
-                weighted = weighted + jnp.sum((p * dp_all[i, block]).reshape(32, 8, 256), axis=0)
-            return total, weighted
-
-        inverse = 1.0 / jnp.sum(sums[0], axis=0, keepdims=True)
-        stats[0, i] = inverse
-        stats[1, i] = jnp.sum(sums[1], axis=0, keepdims=True) * inverse
+        send(lats.at[z, x], lats.at[z, x], s_lat.at[o - 1], r_lat.at[4 * z + x], 4 * at_x(o) + quarter)
+    for o in range(4):
+        scores(at_x(o), y, at_x(2), o == 2)
+    take_core(3, far)
+
+    for n in range(2):
+        scores(at_x(3), far, at_x(2 * n))
+        scores(at_x(3), far, at_x(2 * n + 1))
+
+    take_y(2, 7)
+    scores(x, far, at_x(2))
+    scores(at_x(1), far, at_x(2))
+    take_core(2, far)
+
+    for n in range(2):
+        scores(at_x(2), far, at_x(2 * n))
+        scores(at_x(2), far, at_x(2 * n + 1))
+
+    for n, o in enumerate((1, 3, 2)):
+        other = at_x(o)
+        wait_recv(lats.at[z, other], r_lat.at[4 * z + other])
+        for m, oz in enumerate((1, 3, 2)):
+            to = 4 * lax.div(head, 4) + lax.rem(z + oz, 4)
+            send_head(
+                lats.at[z, other], lats.at[z, other], s_lat.at[3 + 3 * n + m],
+                r_lat.at[4 * z + other], to,
+            )
+
+    for i in range(4):
+        top = stats[0, i, 0]
+        for slot in range(1, 8):
+            top = jnp.maximum(top, stats[0, i, slot])
+        total = jnp.zeros((1, 256), F32)
+        weighted = jnp.zeros((1, 256), F32)
+        for slot in range(8):
+            factor = jnp.exp2(stats[0, i, slot] - top)
+            stats[0, i, slot] = factor
+            total = total + stats[1, i, slot] * factor
+            weighted = weighted + stats[2, i, slot] * factor
+        inverse = 1.0 / total
+        for slot in range(8):
+            stats[0, i, slot] = stats[0, i, slot] * inverse
+        stats[1, i, 0] = weighted * inverse
         dqt[i] = jnp.zeros((256, 256), F32)
-
-    def grads(first, second):
+    wsum[...] = jnp.zeros((512, 256), F32)
+
+    def grads(slot, first, second):
         blocks = (first, second)
         dk = [jnp.zeros((256, 256), F32)] * 2
         dv = [jnp.zeros((256, 128), F32)] * 2
         for i in range(4):
-            inverse, delta = stats[0, i], stats[1, i]
+            inverse, delta = stats[0, i, slot], stats[1, i, 0]
             queries = jnp.concatenate([qd[i, 0:256, :], qm[i]], axis=1)
             ds = []
             for n, block in enumerate(blocks):
@@ -314,22 +378,44 @@
 
     def pass_far(other):
         wait_recv(rc.at[other], r_c.at[other])
-        mine = dkv[4 * other + 2 * (1 - y) + core].astype(F32)
+        mine = dkv[4 * other + 2 * far + core].astype(F32)
         sy[other] = (mine + rc[other].astype(F32)).astype(BF16)
         to_y(other).start()
 
-    @pl.loop(0, 8)
+    def whole_block(other):
+        wait_recv(rc.at[4 + other], r_c.at[4 + other])
+        block = 4 * other + 2 * y + core
+        near = dkv[block].astype(F32) + rc[4 + other].astype(F32)
+        wait_recv(ry.at[other], r_y.at[other])
+        full = (near + ry[other].astype(F32)).astype(BF16)
+        dkv[block] = full
+        return block, full
+
+    def weight_term(other):
+        block = 4 * other + 2 * y + core
+        pair = jnp.concatenate([dkv[block, 0:256, :], dkv[block, 256:512, :]], axis=1)
+        wsum[...] += lax.dot_general(latent_rows(other), pair, TN, preferred_element_type=F32)
+
+    def to_x(n, other, block):
+        return remote(dkv.at[block], rx.at[x], s_x.at[n], r_x.at[x], 4 * other + quarter)
+
+    def give_block(n):
+        other = at_x(n + 1)
+        block, _ = whole_block(other)
+        to_x(n, other, block).start()
+
+    @pl.loop(0, 4)
     def _(n):
-        near = lax.div(n, 4)
-        other = at_x(1 + lax.rem(n, 4))
-        side = near * y + (1 - near) * (1 - y)
-        out = 4 * other + 2 * side + (1 - core)
-        grads(out, 4 * other + 2 * side + core)
-        to_core(4 * near + other, out).start()
-
-        @pl.when((n > 0) & (n < 5))
+        other = at_x(1 + n)
+        grads(2 * other + far, 4 * other + 2 * far + (1 - core), 4 * other + 2 * far + core)
+        to_core(other, 4 * other + 2 * far + (1 - core)).start()
+        grads(2 * other + y, 4 * other + 2 * y + (1 - core), 4 * other + 2 * y + core)
+        to_core(4 + other, 4 * other + 2 * y + (1 - core)).start()
+        pass_far(other)
+
+        @pl.when(n > 0)
         def _():
-            pass_far(at_x(n))
+            give_block(n - 1)
 
     for i in range(4):
         whole = dqt[i].T * SCALE
@@ -337,40 +423,8 @@
         tail = whole[:, 128:256]
         sdq[i, 256:384, :] = jnp.where(low, tail[0:128], swap_halves(tail[128:256])).astype(BF16)
     rdq[x] = sdq[x]
-
-    for o in (1, 2, 3, 0):
-        other = at_x(o)
-        wait_recv(rc.at[4 + other], r_c.at[4 + other])
-        block = 4 * other + 2 * y + core
-        near = dkv[block].astype(F32) + rc[4 + other].astype(F32)
-        wait_recv(ry.at[other], r_y.at[other])
-        full = (near + ry[other].astype(F32)).astype(BF16)
-        dkv[block] = full
-        if o:
-            send(dkv.at[block], rx.at[x], s_x.at[o - 1], r_x.at[x], 4 * other + quarter)
-            wait_recv(lats.at[other], r_lat.at[other])
-        else:
-            rx[x] = full
-        pair = jnp.concatenate([full[0:256], full[256:512]], axis=1)
-        term = lax.dot_general(lats[other], pair, TN, preferred_element_type=F32)
-        if o == 1:
-            wsum[...] = term
-        elif o:
-            wsum[...] += term
-        else:
-            total = (wsum[...] + term).astype(BF16)
-        if o == 3:
-            for oo in (1, 3, 2):
-                send(
-                    sdq.at[at_x(oo)], rdq.at[x], s_dq.at[oo - 1], r_dq.at[x], 4 * at_x(oo) + quarter
-                )
-
-    for cc in range(2):
-        for yy in range(2):
-            for xx in range(4):
-                row = 32 * (4 * xx + 2 * yy + cc)
-                gp[cc, yy, xx] = total[row : row + 32]
-    send(gp.at[1 - core], gc, s_g.at[0], r_g.at[0], core_mate)
+    for o in (1, 3, 2):
+        send(sdq.at[at_x(o)], rdq.at[x], s_dq.at[o - 1], r_dq.at[x], 4 * at_x(o) + quarter)
 
     def latent_term(h):
         columns = pl.ds(pl.multiple_of(128 * h, 128), 128)
@@ -379,10 +433,14 @@
             rx[h, 256:512, :], uv[:, columns], NT, preferred_element_type=F32
         )
 
-    summed = latent_term(x)
-    turned = rx[x, 512:640, :].astype(F32)
-    for o in (3, 2, 1):
-        wait_recv(rx.at[at_x(o)], r_x.at[at_x(o)])
+    summed = jnp.zeros((256, 512), F32)
+    turned = jnp.zeros((128, 128), F32)
+    for o in (3, 2, 0, 1):
+        if o:
+            wait_recv(rx.at[at_x(o)], r_x.at[at_x(o)])
+        else:
+            _, full = whole_block(x)
+            rx[x] = full
         summed = summed + latent_term(at_x(o))
         turned = turned + rx[at_x(o), 512:640, :].astype(F32)
     half = piece // 2
@@ -391,22 +449,24 @@
         sl[p, 0:half, 512:640] = turned[half * p : half * p + half].astype(BF16)
         sl[p, half:piece, 512:640] = jnp.zeros((piece - half, 128), BF16)
 
-    def send_head(src, dst, send_sem, recv_sem, to):
-        copy = pltpu.make_async_remote_copy(
-            src_ref=src,
-            dst_ref=dst,
-            send_sem=send_sem,
-            recv_sem=recv_sem,
-            device_id={"head": to},
-            device_id_type=MESH,
-        )
-        copy.start()
-        started.append(copy)
-
     for o in range(1, heads):
         to = lax.rem(head + o, heads)
         send_head(sl.at[to], rl.at[head], s_l.at[o], r_l.at[head], to)
     rl[head] = sl[head]
+
+    for o in (1, 2, 3, 0):
+        if o:
+            for oz in (1, 2, 3):
+                part = lax.rem(z + oz, 4)
+                wait_recv(lats.at[part, at_x(o)], r_lat.at[4 * part + at_x(o)])
+        weight_term(at_x(o))
+    total = wsum[...].astype(BF16)
+    for cc in range(2):
+        for yy in range(2):
+            for xx in range(4):
+                row = 32 * (4 * xx + 2 * yy + cc)
+                gp[cc, yy, xx] = total[row : row + 32]
+    send(gp.at[1 - core], gc, s_g.at[0], r_g.at[0], core_mate)
 
     wait_recv(gc, r_g.at[0])
     sgy[...] = (gp[core, 1 - y].astype(F32) + gc[1 - y].astype(F32)).astype(BF16)
@@ -461,9 +521,12 @@
     for copy in started:
         copy.wait_send()
     for other in range(4):
-        to_y(other).wait_send()
         to_core(other, other).wait_send()
         to_core(4 + other, other).wait_send()
+    for n in range(4):
+        to_y(n).wait_send()
+    for n in range(3):
+        to_x(n, at_x(n + 1), 0).wait_send()
 
 
 def fused(heads, order, qn, qr, og, lat, rope_t, uk, uv):
@@ -489,10 +552,10 @@
         scratch_shapes=[
             bf(256, 512), bf(256, 256), bf(256, 512), bf(64, 256), bf(512, 512), bf(512, 512),
             bf(4, ROWS, 128), bf(4, ROWS, 128), bf(BLOCKS, ROWS, 128), bf(4, ROWS, 128),
-            bf(4, 256, 512),
+            bf(4, 4, 256, 128),
             bf(BLOCKS, 256, 128), bf(BLOCKS, 256, 256), bf(4, 256, 128), bf(4, 256, 256),
             bf(4, 128, 256),
-            f32(4, BLOCKS, 256, 256), f32(4, BLOCKS, 256, 256), f32(4, 8, 256), f32(2, 4, 1, 256),
+            f32(4, BLOCKS, 256, 256), f32(4, BLOCKS, 256, 256), f32(3, 4, 8, 1, 256),
             f32(4, 256, 256),
             bf(BLOCKS, ROWS, 128), bf(8, ROWS, 128), bf(4, ROWS, 128), bf(4, ROWS, 128),
             bf(4, ROWS, 128), bf(4, DQ_ROWS, 128), bf(4, DQ_ROWS, 128),
@@ -500,8 +563,8 @@
             bf(2, 2, 4, 32, 256), bf(2, 4, 32, 256), bf(4, 32, 256), bf(4, 32, 256),
             bf(4, 32, 256), bf(4, 32, 256),
             bf(heads, piece, 640), bf(heads, piece, 640), bf(heads, piece, 640),
-            dma((7,)), dma((3,)), dma((4,)), dma((8,)), dma((BLOCKS,)), dma((3,)), dma((4,)),
-            dma((3,)), dma((4,)),
+            dma((10,)), dma((6,)), dma((8,)), dma((16,)), dma((2 * BLOCKS,)), dma((3,)), dma((4,)),
+            dma((12,)), dma((16,)),
             dma((8,)), dma((8,)), dma((4,)), dma((4,)), dma((3,)), dma((4,)), dma((3,)), dma((4,)),
             dma((2,)), dma((2,)), dma((3,)), dma((4,)),
             dma((heads,)), dma((heads,)), dma((heads,)), dma((heads,)),

time: 73.8 us -> 70.8 us (0.959)
  Pallas kernels: 73 us -> 69.8 us
    pallas_call x1, Pallas kernels: 70.7 us -> 67.6 us  [fused(): pl.pallas_call(functools.partial(fused_kernel, heads), name='fused', out_...]
where the time goes in v3:
time: 70.8 us; the launch traced here: 70.6 us
  Pallas kernels  69.8 us (99%)
  between operations  0.8 us (1%)
    pallas_call x1, Pallas kernels, fused(): pl.pallas_call(functools.partial(fused_kernel, heads), name='fused', out_...  67.6 us
    pallas_call x1, Pallas kernels, finish(): pl.pallas_call(finish_kernel, name='finish', out_shape=tuple((jax.ShapeDt...  2.26 us

profile of v3, /device:TPU:0, one launch (start us, length us, event | category | flops | bytes accessed | tf_op | source)
XLA Modules:
  0.0 70.6 jit_solution(14012897351914003122)
XLA Ops:
  0.6 67.6 %fused.1 = (bf16[256,512]{1,0:T(8,128)(2,1)}, bf16[256,256]{1,0:T(8,128)(2,1)}, f32[256,512]{1,0:T(8,128)}, f32[64,256]{1,0:T(8,128)}, f32[32,512]{1,0:T(8,128)}, /*index=5*/f32[32,512]{1,0:T(8,128)}) custom-call(s32[32]{0:T(128)} %order.1, bf16[256,512]{1,0:T(8,128)(2,1)} %qn_in.1, bf16[256,256]{1,0:T(8,128)(2,1)} %qr_in.1, bf16[256,512]{1,0:T(8,128)(2,1)} %og_in.1, ...), custom_call_target="tpu_custom_call" | custom-call | tf_op jit(solution)/shard_map/fused/pallas_call | solution.py:539
  68.2 2.3 %finish.1 = (bf16[256,512]{1,0:T(8,128)(2,1)}, bf16[256,256]{1,0:T(8,128)(2,1)}, f32[256,512]{1,0:T(8,128)}, f32[64,256]{1,0:T(8,128)}, f32[32,512]{1,0:T(8,128)}, /*index=5*/f32[32,512]{1,0:T(8,128)}) custom-call(bf16[256,512]{1,0:T(8,128)(2,1)} %get-tuple-element.18.refs_0_, bf16[256,256]{1,0:T(8,128)(2,1)} %get-tuple-element.19.refs_1_, ...), custom_call_target="tpu_custom_call" | custom-call | tf_op jit(solution)/shard_map/finish/pallas_call | solution.py:592

commit v4 on v3

--- a/solution.py
+++ b/solution.py
@@ -62,9 +62,9 @@
     gqn, gqr, gl, gr, guk, guv,
     qn, qr, og, rope, uk, uv, skv, sq, kv, qd, lats,
     rm, kt, qm, qct, doct, s_all, dp_all, stats, dqt,
-    dkv, rc, sy, ry, rx, sdq, rdq, wsum, gp, gc, sgy, rgy, sgx, rgx, sl, rl, ag,
+    dkv, rc, sy, ry, rf, sfr, rfr, rx, sdq, rdq, wsum, gp, gc, sgy, rgy, sgx, rgx, sl, rl, ag,
     load_sem, s_kvx, s_kvy, s_kvc, r_kv, s_q, r_q, s_lat, r_lat,
-    s_c, r_c, s_y, r_y, s_x, r_x, s_dq, r_dq, s_g, r_g, s_gx, r_gx, s_l, r_l, s_a, r_a,
+    s_c, r_c, s_y, r_y, s_f, r_f, s_fr, r_fr, s_x, r_x, s_dq, r_dq, s_g, r_g, s_gx, r_gx, s_l, r_l, s_a, r_a,
 ):
     me = lax.axis_index("ctx")
     head = lax.axis_index("head")
@@ -373,23 +373,36 @@
     def to_core(slot, block):
         return remote(dkv.at[block], rc.at[slot], s_c.at[slot], r_c.at[slot], core_mate)
 
+    turned_rows = pl.ds(512, 128)
+
     def to_y(other):
-        return remote(sy.at[other], ry.at[other], s_y.at[other], r_y.at[other], y_mate)
-
-    def pass_far(other):
+        return remote(
+            sy.at[other, pl.ds(0, 512)], ry.at[other], s_y.at[other], r_y.at[other], y_mate
+        )
+
+    def to_far_x(n, other):
+        return remote(
+            sy.at[other, turned_rows], rf.at[x], s_f.at[n], r_f.at[x], 4 * other + quarter
+        )
+
+    def pass_far(n, other):
         wait_recv(rc.at[other], r_c.at[other])
         mine = dkv[4 * other + 2 * far + core].astype(F32)
         sy[other] = (mine + rc[other].astype(F32)).astype(BF16)
         to_y(other).start()
+
+        @pl.when(n < 3)
+        def _():
+            to_far_x(n, other).start()
 
     def whole_block(other):
         wait_recv(rc.at[4 + other], r_c.at[4 + other])
         block = 4 * other + 2 * y + core
         near = dkv[block].astype(F32) + rc[4 + other].astype(F32)
         wait_recv(ry.at[other], r_y.at[other])
-        full = (near + ry[other].astype(F32)).astype(BF16)
-        dkv[block] = full
-        return block, full
+        dkv[block, 0:512, :] = (near[0:512] + ry[other].astype(F32)).astype(BF16)
+        dkv[block, 512:640, :] = near[512:640].astype(BF16)
+        return block
 
     def weight_term(other):
         block = 4 * other + 2 * y + core
@@ -401,7 +414,7 @@
 
     def give_block(n):
         other = at_x(n + 1)
-        block, _ = whole_block(other)
+        block = whole_block(other)
         to_x(n, other, block).start()
 
     @pl.loop(0, 4)
@@ -411,12 +424,18 @@
         to_core(other, 4 * other + 2 * far + (1 - core)).start()
         grads(2 * other + y, 4 * other + 2 * y + (1 - core), 4 * other + 2 * y + core)
         to_core(4 + other, 4 * other + 2 * y + (1 - core)).start()
-        pass_far(other)
+        pass_far(n, other)
 
         @pl.when(n > 0)
         def _():
             give_block(n - 1)
 
+    far_turned = sy[x, 512:640, :].astype(F32)
+    for o in (3, 2, 1):
+        wait_recv(rf.at[at_x(o)], r_f.at[at_x(o)])
+        far_turned = far_turned + rf[at_x(o)].astype(F32)
+    sfr[...] = far_turned.astype(BF16)
+    send(sfr, rfr, s_fr.at[0], r_fr.at[0], y_mate)
     for i in range(4):
         whole = dqt[i].T * SCALE
         sdq[i, 0:256, :] = whole[:, 0:128].astype(BF16)
@@ -439,10 +458,11 @@
         if o:
             wait_recv(rx.at[at_x(o)], r_x.at[at_x(o)])
         else:
-            _, full = whole_block(x)
-            rx[x] = full
+            rx[x] = dkv[whole_block(x)]
         summed = summed + latent_term(at_x(o))
         turned = turned + rx[at_x(o), 512:640, :].astype(F32)
+    wait_recv(rfr, r_fr.at[0])
+    turned = turned + rfr[...].astype(F32)
     half = piece // 2
     for p in range(heads):
         sl[p, :, 0:512] = summed[piece * p : piece * p + piece].astype(BF16)
@@ -527,6 +547,7 @@
         to_y(n).wait_send()
     for n in range(3):
         to_x(n, at_x(n + 1), 0).wait_send()
+        to_far_x(n, at_x(n + 1)).wait_send()
 
 
 def fused(heads, order, qn, qr, og, lat, rope_t, uk, uv):
@@ -557,15 +578,16 @@
             bf(4, 128, 256),
             f32(4, BLOCKS, 256, 256), f32(4, BLOCKS, 256, 256), f32(3, 4, 8, 1, 256),
             f32(4, 256, 256),
-            bf(BLOCKS, ROWS, 128), bf(8, ROWS, 128), bf(4, ROWS, 128), bf(4, ROWS, 128),
-            bf(4, ROWS, 128), bf(4, DQ_ROWS, 128), bf(4, DQ_ROWS, 128),
+            bf(BLOCKS, ROWS, 128), bf(8, ROWS, 128), bf(4, ROWS, 128), bf(4, 512, 128),
+            bf(4, 128, 128), bf(128, 128), bf(128, 128), bf(4, ROWS, 128), bf(4, DQ_ROWS, 128), bf(4, DQ_ROWS, 128),
             f32(512, 256),
             bf(2, 2, 4, 32, 256), bf(2, 4, 32, 256), bf(4, 32, 256), bf(4, 32, 256),
             bf(4, 32, 256), bf(4, 32, 256),
             bf(heads, piece, 640), bf(heads, piece, 640), bf(heads, piece, 640),
             dma((10,)), dma((6,)), dma((8,)), dma((16,)), dma((2 * BLOCKS,)), dma((3,)), dma((4,)),
             dma((12,)), dma((16,)),
-            dma((8,)), dma((8,)), dma((4,)), dma((4,)), dma((3,)), dma((4,)), dma((3,)), dma((4,)),
+            dma((8,)), dma((8,)), dma((4,)), dma((4,)), dma((4,)), dma((4,)), dma((1,)), dma((1,)),
+            dma((3,)), dma((4,)), dma((3,)), dma((4,)),
             dma((2,)), dma((2,)), dma((3,)), dma((4,)),
             dma((heads,)), dma((heads,)), dma((heads,)), dma((heads,)),
         ],

time: 70.8 us -> 69.5 us (0.982)
  Pallas kernels: 69.8 us -> 68.6 us
    pallas_call x1, Pallas kernels: 67.6 us -> 66.3 us  [fused(): pl.pallas_call(functools.partial(fused_kernel, heads), name='fused', out_...]
where the time goes in v4:
time: 69.5 us; the launch traced here: 69.4 us
  Pallas kernels  68.6 us (99%)
  between operations  0.8 us (1%)
    pallas_call x1, Pallas kernels, fused(): pl.pallas_call(functools.partial(fused_kernel, heads), name='fused', out_...  66.3 us
    pallas_call x1, Pallas kernels, finish(): pl.pallas_call(finish_kernel, name='finish', out_shape=tuple((jax.ShapeDt...  2.26 us

profile of v4, /device:TPU:0, one launch (start us, length us, event | category | flops | bytes accessed | tf_op | source)
XLA Modules:
  0.0 69.4 jit_solution(657877345700852992)
XLA Ops:
  0.6 66.3 %fused.1 = (bf16[256,512]{1,0:T(8,128)(2,1)}, bf16[256,256]{1,0:T(8,128)(2,1)}, f32[256,512]{1,0:T(8,128)}, f32[64,256]{1,0:T(8,128)}, f32[32,512]{1,0:T(8,128)}, /*index=5*/f32[32,512]{1,0:T(8,128)}) custom-call(s32[32]{0:T(128)} %order.1, bf16[256,512]{1,0:T(8,128)(2,1)} %qn_in.1, bf16[256,256]{1,0:T(8,128)(2,1)} %qr_in.1, bf16[256,512]{1,0:T(8,128)(2,1)} %og_in.1, ...), custom_call_target="tpu_custom_call" | custom-call | tf_op jit(solution)/shard_map/fused/pallas_call | solution.py:560
  66.9 2.3 %finish.1 = (bf16[256,512]{1,0:T(8,128)(2,1)}, bf16[256,256]{1,0:T(8,128)(2,1)}, f32[256,512]{1,0:T(8,128)}, f32[64,256]{1,0:T(8,128)}, f32[32,512]{1,0:T(8,128)}, /*index=5*/f32[32,512]{1,0:T(8,128)}) custom-call(bf16[256,512]{1,0:T(8,128)(2,1)} %get-tuple-element.18.refs_0_, bf16[256,256]{1,0:T(8,128)(2,1)} %get-tuple-element.19.refs_1_, ...), custom_call_target="tpu_custom_call" | custom-call | tf_op jit(solution)/shard_map/finish/pallas_call | solution.py:614

commit v5 on v4

--- a/solution.py
+++ b/solution.py
@@ -98,6 +98,11 @@
         pl.semaphore_signal(
             barrier, inc=1, device_id={"head": lax.rem(head + o, heads)}, device_id_type=MESH
         )
+
+    far_first = (6, 5, 7, 4, 2, 1, 3)
+
+    def head_peer(o):
+        return 4 * lax.rem(lax.div(head, 4) + o // 4, 2) + lax.rem(z + o % 4, 4)
 
     started = []
 
@@ -391,8 +396,7 @@
         sy[other] = (mine + rc[other].astype(F32)).astype(BF16)
         to_y(other).start()
 
-        @pl.when(n < 3)
-        def _():
+        if n < 3:
             to_far_x(n, other).start()
 
     def whole_block(other):
@@ -417,8 +421,7 @@
         block = whole_block(other)
         to_x(n, other, block).start()
 
-    @pl.loop(0, 4)
-    def _(n):
+    for n in range(4):
         other = at_x(1 + n)
         grads(2 * other + far, 4 * other + 2 * far + (1 - core), 4 * other + 2 * far + core)
         to_core(other, 4 * other + 2 * far + (1 - core)).start()
@@ -426,8 +429,7 @@
         to_core(4 + other, 4 * other + 2 * y + (1 - core)).start()
         pass_far(n, other)
 
-        @pl.when(n > 0)
-        def _():
+        if n > 0:
             give_block(n - 1)
 
     far_turned = sy[x, 512:640, :].astype(F32)
@@ -442,8 +444,6 @@
         tail = whole[:, 128:256]
         sdq[i, 256:384, :] = jnp.where(low, tail[0:128], swap_halves(tail[128:256])).astype(BF16)
     rdq[x] = sdq[x]
-    for o in (1, 3, 2):
-        send(sdq.at[at_x(o)], rdq.at[x], s_dq.at[o - 1], r_dq.at[x], 4 * at_x(o) + quarter)
 
     def latent_term(h):
         columns = pl.ds(pl.multiple_of(128 * h, 128), 128)
@@ -469,9 +469,11 @@
         sl[p, 0:half, 512:640] = turned[half * p : half * p + half].astype(BF16)
         sl[p, half:piece, 512:640] = jnp.zeros((piece - half, 128), BF16)
 
-    for o in range(1, heads):
-        to = lax.rem(head + o, heads)
+    for o in far_first:
+        to = head_peer(o)
         send_head(sl.at[to], rl.at[head], s_l.at[o], r_l.at[head], to)
+    for o in (1, 3, 2):
+        send(sdq.at[at_x(o)], rdq.at[x], s_dq.at[o - 1], r_dq.at[x], 4 * at_x(o) + quarter)
     rl[head] = sl[head]
 
     for o in (1, 2, 3, 0):
@@ -493,6 +495,17 @@
     send(sgy, rgy, s_g.at[1], r_g.at[1], y_mate)
     near_g = gp[core, y].astype(F32) + gc[y].astype(F32)
 
+    for o in range(1, heads):
+        source = lax.rem(head + o, heads)
+        wait_recv(rl.at[source], r_l.at[source])
+    over_heads = rl[0].astype(F32)
+    for p in range(1, heads):
+        over_heads = over_heads + rl[p].astype(F32)
+    ag[head] = over_heads.astype(BF16)
+    for o in far_first:
+        to = head_peer(o)
+        send_head(ag.at[head], ag.at[head], s_a.at[o], r_a.at[head], to)
+
     for o in (1, 2, 3):
         wait_recv(rdq.at[at_x(o)], r_dq.at[at_x(o)])
     for h in range(4):
@@ -509,17 +522,6 @@
     for o in (1, 3, 2):
         send(sgx.at[at_x(o)], rgx.at[x], s_gx.at[o - 1], r_gx.at[x], 4 * at_x(o) + quarter)
     rgx[x] = sgx[x]
-
-    for o in range(1, heads):
-        source = lax.rem(head + o, heads)
-        wait_recv(rl.at[source], r_l.at[source])
-    over_heads = rl[0].astype(F32)
-    for p in range(1, heads):
-        over_heads = over_heads + rl[p].astype(F32)
-    ag[head] = over_heads.astype(BF16)
-    for o in range(1, heads):
-        to = lax.rem(head + o, heads)
-        send_head(ag.at[head], ag.at[head], s_a.at[o], r_a.at[head], to)
 
     for o in (1, 2, 3):
         wait_recv(rgx.at[at_x(o)], r_gx.at[at_x(o)])

time: 69.5 us -> 68.2 us (0.981)
  Pallas kernels: 68.6 us -> 66.9 us
    pallas_call x1, Pallas kernels: 66.3 us -> 64.6 us  [fused(): pl.pallas_call(functools.partial(fused_kernel, heads), name='fused', out_...]
where the time goes in v5:
time: 68.2 us; the launch traced here: 67.7 us
  Pallas kernels  66.9 us (98%)
  between operations  0.8 us (1%)
    pallas_call x1, Pallas kernels, fused(): pl.pallas_call(functools.partial(fused_kernel, heads), name='fused', out_...  64.6 us
    pallas_call x1, Pallas kernels, finish(): pl.pallas_call(finish_kernel, name='finish', out_shape=tuple((jax.ShapeDt...  2.26 us

profile of v5, /device:TPU:0, one launch (start us, length us, event | category | flops | bytes accessed | tf_op | source)
XLA Modules:
  0.0 67.7 jit_solution(8678044081197151666)
XLA Ops:
  0.6 64.6 %fused.1 = (bf16[256,512]{1,0:T(8,128)(2,1)}, bf16[256,256]{1,0:T(8,128)(2,1)}, f32[256,512]{1,0:T(8,128)}, f32[64,256]{1,0:T(8,128)}, f32[32,512]{1,0:T(8,128)}, /*index=5*/f32[32,512]{1,0:T(8,128)}) custom-call(s32[32]{0:T(128)} %order.1, bf16[256,512]{1,0:T(8,128)(2,1)} %qn_in.1, bf16[256,256]{1,0:T(8,128)(2,1)} %qr_in.1, bf16[256,512]{1,0:T(8,128)(2,1)} %og_in.1, ...), custom_call_target="tpu_custom_call" | custom-call | tf_op jit(solution)/shard_map/fused/pallas_call | solution.py:562
  65.3 2.3 %finish.1 = (bf16[256,512]{1,0:T(8,128)(2,1)}, bf16[256,256]{1,0:T(8,128)(2,1)}, f32[256,512]{1,0:T(8,128)}, f32[64,256]{1,0:T(8,128)}, f32[32,512]{1,0:T(8,128)}, /*index=5*/f32[32,512]{1,0:T(8,128)}) custom-call(bf16[256,512]{1,0:T(8,128)(2,1)} %get-tuple-element.18.refs_0_, bf16[256,256]{1,0:T(8,128)(2,1)} %get-tuple-element.19.refs_1_, ...), custom_call_target="tpu_custom_call" | custom-call | tf_op jit(solution)/shard_map/finish/pallas_call | solution.py:616
